TPU v7x, 768 devices: a whole 4x8x12 slice. The times are simulated.
768 devices in a mesh: dom: 64 (over y, x, core), sub: 12 (over z).
Axes of the slice: x: 4, y: 8, z: 12, core: 2. Of those that a mesh axis runs over, the one named last changes fastest.
Arguments:
- geometry: bfloat16 [6, 512, 98304], P(None, None, ('dom', 'sub')), may hold values from -1.8 to 4, as said below
- load: float32 [512, 98304], P(None, ('dom', 'sub')), may hold values from -600 to 600
- cells: int32 [768, 128], P(('dom', 'sub')), may hold values from 0 to 127, each once within a row
Outputs:
- smoothed: float32 [512, 98304], P(None, ('dom', 'sub'))
Inputs may be any that keep to these rules, and one draw needn't show every extreme that they name: `geometry`: at each node the matrix [[g0, g3, g4], [g3, g1, g5], [g4, g5, g2]] is symmetric positive definite.
All inputs are finite; a program needn't handle non-finite values.
Results may differ from a plain program's by a relative error of at most 0.0003.
Values sent between devices are 32-bit elements; how exact they have to be, the bound alone decides.
No kernel may reach another device: no remote copies, remote signals or barrier semaphores. Data moves between devices by JAX's collectives and lax.ppermute only.
A program may use at most 128 MiB of HBM per device.

v0:
```python
import functools

import jax
import jax.numpy as jnp
import ml_dtypes
import numpy as np
from jax import lax
from jax.experimental import pallas as pl
from jax.experimental.pallas import tpu as pltpu
from jax.sharding import PartitionSpec as P

NP = 8
APPLY = 4
LANES = 128
ROWS = NP**3

cheb_low = 0.4
cheb_high = 4.0


def legendre_values(points, degree):
    before = np.ones(points.shape[0])
    current = points.copy()
    for order in range(2, degree + 1):
        following = ((2 * order - 1) * points * current - (order - 1) * before) / order
        before = current
        current = following
    return (current, before)


def derivative_table(number):
    degree = number - 1
    points = np.cos(np.pi * np.arange(degree + 1) / degree)
    for sweep in range(60):
        current, before = legendre_values(points, degree)
        inner = points[1:-1]
        step_size = (inner * current[1:-1] - before[1:-1]) / ((degree + 1) * current[1:-1])
        points = np.concatenate([points[:1], inner - step_size, points[-1:]])
    points = np.sort(points)
    points = np.concatenate([np.zeros(1) - 1.0, points[1:-1], np.zeros(1) + 1.0])
    values, unused = legendre_values(points, degree)
    matrix = np.zeros((number, number))
    for row_index in range(number):
        for col_index in range(number):
            if row_index != col_index:
                matrix[row_index, col_index] = values[row_index] / (
                    values[col_index] * (points[row_index] - points[col_index])
                )
    matrix[0, 0] = -degree * (degree + 1) / 4.0
    matrix[degree, degree] = degree * (degree + 1) / 4.0
    return matrix


def three_products(matrix):
    matrix = matrix.astype(np.float32)
    high = matrix.astype(ml_dtypes.bfloat16)
    low = (matrix - high.astype(np.float32)).astype(ml_dtypes.bfloat16)
    return np.concatenate([high, high, low], axis=1)


def tables():
    derivative = derivative_table(NP).astype(np.float32).astype(np.float64)
    eye = np.eye(NP)
    outer = three_products(np.kron(derivative, eye))
    inner = three_products(np.kron(eye, derivative))
    outer_t = three_products(np.kron(derivative.T, eye))
    inner_t = three_products(np.kron(eye, derivative.T))
    apply_table = np.concatenate([outer, inner, outer_t, inner_t], axis=0)
    square = derivative * derivative
    diag_table = np.concatenate(
        [three_products(np.kron(square.T, eye)), three_products(np.kron(eye, square.T))], axis=0
    )
    return apply_table, diag_table, np.diagonal(derivative)


def split_rows(values):
    high = values.astype(jnp.bfloat16)
    low = (values - high.astype(jnp.float32)).astype(jnp.bfloat16)
    return jnp.concatenate([high, low, high], axis=0)


def multiply(left, right):
    return jnp.dot(left, right, preferred_element_type=jnp.float32)


def gather_first(ref, j):
    return jnp.concatenate([ref[i * 64 + j * 8 : i * 64 + j * 8 + 8, :] for i in range(NP)], axis=0)


def lane_of(rows):
    return lax.broadcasted_iota(jnp.int32, (rows, LANES), 1)


def join_pair(low_face, high_face, lane, unit, number):
    coordinate = (lane // unit) % number
    new_low = low_face + jnp.where(coordinate > 0, pltpu.roll(high_face, unit, 1), 0.0)
    new_high = high_face + jnp.where(
        coordinate < number - 1, pltpu.roll(low_face, LANES - unit, 1), 0.0
    )
    return new_low, new_high


def join_local(ref):
    lane8 = lane_of(8)
    lane64 = lane_of(64)
    for i in range(NP):
        first = slice(i * 64, i * 64 + 8)
        last = slice(i * 64 + 56, i * 64 + 64)
        ref[first, :], ref[last, :] = join_pair(ref[first, :], ref[last, :], lane8, 8, 4)
    ref[0:64, :], ref[448:512, :] = join_pair(ref[0:64, :], ref[448:512, :], lane64, 32, 4)
    first = pl.ds(0, 64, stride=8)
    last = pl.ds(7, 64, stride=8)
    new_first, new_last = join_pair(ref[first, :], ref[last, :], lane64, 1, 8)
    ref[first, :] = new_first
    ref[last, :] = new_last


class Side:
    def __init__(self, sizes, stage):
        a = lax.axis_index("dom")
        b = lax.axis_index("sub")
        self.lr = lax.rem(a + stage, 2)
        self.ls = lax.rem(b + stage, 2)
        self.place = 2 * self.lr + self.ls
        self.dom_slot = 2 * (1 - self.lr) + self.ls
        self.sub_slot = 2 * self.lr + (1 - self.ls)
        self.far_slot = 3 - self.place
        self.vr = None
        self.vs = None
        if stage:
            self.vr = jnp.where(self.lr == 1, a > 0, a < sizes[0] - 1)
            self.vs = jnp.where(self.ls == 1, b > 0, b < sizes[1] - 1)
        self.i_row = pl.multiple_of((1 - self.lr) * 448, 64)
        self.j_row = (1 - self.ls) * 56


def keep(mask, *conditions):
    for condition in conditions:
        if condition is not None:
            mask = jnp.logical_and(mask, condition)
    return mask


def pack_faces(ref, side):
    lane = lane_of(16)
    dom_face = jnp.zeros((16, LANES), jnp.float32)
    sub_face = jnp.zeros((16, LANES), jnp.float32)
    for g in range(4):
        block = ref[pl.ds(pl.multiple_of(side.i_row + g * 16, 8), 16), :]
        shift = (g * 32 + 32 * (1 - side.lr)) & 127
        dom_face = jnp.where(lane // 32 == g, pltpu.roll(block, shift, 1), dom_face)
        block = jnp.concatenate(
            [
                ref[pl.ds(pl.multiple_of(i * 64 + side.j_row, 8), 8), :]
                for i in (2 * g, 2 * g + 1)
            ],
            axis=0,
        )
        shift = (g * 8 + 128 - 24 * (1 - side.ls)) & 127
        sub_face = jnp.where((lane // 8) % 4 == g, pltpu.roll(block, shift, 1), sub_face)
    corner = ref[pl.ds(pl.multiple_of(side.i_row + side.j_row, 8), 8), :]
    return dom_face, sub_face, corner


def write_faces(out_ref, field, faces, side):
    dom_face, sub_face, corner = faces
    row = field * 16
    out_ref[side.dom_slot, row : row + 16, :] = dom_face
    out_ref[side.sub_slot, row : row + 16, :] = sub_face
    out_ref[side.far_slot, row : row + 8, :] = corner
    out_ref[side.far_slot, row + 8 : row + 16, :] = jnp.zeros((8, LANES), jnp.float32)
    out_ref[side.place, row : row + 16, :] = jnp.zeros((16, LANES), jnp.float32)


def add_faces(ref, recv_ref, field, side):
    lane = lane_of(16)
    lane8 = lane_of(8)
    row = field * 16
    dom_face = recv_ref[side.dom_slot, row : row + 16, :]
    for g in range(4):
        shift = (96 * (1 - side.lr) + 128 - g * 32) & 127
        mask = keep(lane // 32 == 3 * (1 - side.lr), side.vr)
        at = pl.ds(pl.multiple_of(side.i_row + g * 16, 8), 16)
        ref[at, :] = ref[at, :] + jnp.where(mask, pltpu.roll(dom_face, shift, 1), 0.0)
    sub_mask = keep((lane8 // 8) % 4 == 3 * (1 - side.ls), side.vs)
    sub_face = recv_ref[side.sub_slot, row : row + 16, :]
    for g in range(4):
        shift = (24 * (1 - side.ls) + 128 - g * 8) & 127
        rolled = pltpu.roll(sub_face, shift, 1)
        for part in range(2):
            at = pl.ds(pl.multiple_of((2 * g + part) * 64 + side.j_row, 8), 8)
            piece = rolled[part * 8 : part * 8 + 8, :]
            ref[at, :] = ref[at, :] + jnp.where(sub_mask, piece, 0.0)
    corner = recv_ref[side.far_slot, row : row + 8, :]
    offset = 96 * (1 - side.lr) + 24 * (1 - side.ls)
    shift = (2 * offset + 256 - 120) & 127
    mask = keep(lane8 // 8 == offset // 8, side.vr, side.vs)
    at = pl.ds(pl.multiple_of(side.i_row + side.j_row, 8), 8)
    ref[at, :] = ref[at, :] + jnp.where(mask, pltpu.roll(corner, shift, 1), 0.0)


def apply_operator(value_ref, geo_ref, table_ref, image_ref, work_ref):
    outer = table_ref[0:64, :]
    both = table_ref[0:128, :]
    outer_t = table_ref[128:192, :]
    inner_t = table_ref[192:256, :]
    for j in range(NP):
        product = multiply(outer, split_rows(gather_first(value_ref, j)))
        for i in range(NP):
            work_ref[i * 64 + j * 8 : i * 64 + j * 8 + 8, :] = product[i * 8 : i * 8 + 8, :]
    for i in range(NP):
        at = slice(i * 64, i * 64 + 64)
        product = multiply(both, split_rows(value_ref[at, :]))
        grad_r = work_ref[at, :]
        grad_s = product[0:64, :]
        grad_t = product[64:128, :]
        g = [geo_ref[index, at, :].astype(jnp.float32) for index in range(6)]
        work_ref[at, :] = g[0] * grad_r + g[3] * grad_s + g[4] * grad_t
        flux_s = g[3] * grad_r + g[1] * grad_s + g[5] * grad_t
        flux_t = g[4] * grad_r + g[5] * grad_s + g[2] * grad_t
        image_ref[at, :] = multiply(outer_t, split_rows(flux_s)) + multiply(
            inner_t, split_rows(flux_t)
        )
    for j in range(NP):
        product = multiply(outer_t, split_rows(gather_first(work_ref, j)))
        for i in range(NP):
            at = slice(i * 64 + j * 8, i * 64 + j * 8 + 8)
            image_ref[at, :] = image_ref[at, :] + product[i * 8 : i * 8 + 8, :]


def emit_faces(ref, field, send_ref, later_ref, sides):
    write_faces(send_ref, field, pack_faces(ref, sides[0]), sides[0])
    write_faces(later_ref, field, pack_faces(ref, sides[1]), sides[1])


def permute_exact(values, table):
    total = None
    for part in range(3):
        piece = values.astype(jnp.bfloat16)
        moved = multiply(piece, table)
        values = values - piece.astype(jnp.float32)
        total = moved if total is None else total + moved
    return total


def begin_kernel(sizes, middle, geo_ref, load_ref, cells_ref, table_ref, geo_out, parts_ref, send_ref, later_ref, work_ref):
    listed = cells_ref[...]
    cell = lax.broadcasted_iota(jnp.int32, (LANES, LANES), 0)
    by_cell = jnp.where(cell == jnp.broadcast_to(listed, (LANES, LANES)), 1.0, 0.0)
    table = by_cell.T.astype(jnp.bfloat16)
    for index in range(6):
        geo_out[index] = multiply(geo_ref[index], table).astype(jnp.bfloat16)
    outer = table_ref[0:64, :]
    inner = table_ref[64:128, :]
    work_ref[...] = geo_out[0].astype(jnp.float32)
    load_part = parts_ref.at[0]
    diag_part = parts_ref.at[1]
    sub_row = lax.broadcasted_iota(jnp.int32, (64, LANES), 0) % 8
    third = jnp.where(sub_row == 0, middle[0], jnp.where(sub_row == 7, middle[7], 0.0))
    for i in range(NP):
        at = slice(i * 64, i * 64 + 64)
        load_part[at, :] = permute_exact(load_ref[at, :], table)
        first = split_rows(geo_out[1, at, :].astype(jnp.float32))
        second = split_rows(geo_out[2, at, :].astype(jnp.float32))
        total = multiply(outer, first) + multiply(inner, second)
        if i in (0, 7):
            total = total + 2.0 * middle[i] * third * geo_out[4, at, :].astype(jnp.float32)
        diag_part[at, :] = total
        for j in (0, 7):
            here = slice(i * 64 + j * 8, i * 64 + j * 8 + 8)
            fifth = geo_out[5, at, :].astype(jnp.float32)[j * 8 : j * 8 + 8, :]
            extra = middle[j] * third[0:8, :] * fifth
            if i in (0, 7):
                cross = geo_out[3, at, :].astype(jnp.float32)[j * 8 : j * 8 + 8, :]
                extra = extra + middle[i] * middle[j] * cross
            diag_part[here, :] = diag_part[here, :] + 2.0 * extra
    for j in range(NP):
        product = multiply(outer, split_rows(gather_first(work_ref, j)))
        for i in range(NP):
            at = slice(i * 64 + j * 8, i * 64 + j * 8 + 8)
            diag_part[at, :] = diag_part[at, :] + product[i * 8 : i * 8 + 8, :]
    sides = (Side(sizes, 0), Side(sizes, 1))
    for field in range(2):
        join_local(parts_ref.at[field])
        emit_faces(parts_ref.at[field], field, send_ref, later_ref, sides)


def middle_kernel(sizes, fields, recv_ref, later_ref, out_ref):
    now = Side(sizes, 0)
    then = Side(sizes, 1)
    out_ref[...] = later_ref[...]
    lane = lane_of(8)
    for field in range(fields):
        row = field * 16

        def correct(slot_in, low_in, slot_out, low_out):
            piece = recv_ref[slot_in, pl.ds(pl.multiple_of(row + 8 * (1 - low_in), 8), 8), :]
            shift = (8 + 128 - 8 * (1 - low_out) + 8 * (1 - low_in) - 8) & 127
            mask = lane // 8 == 15 * (1 - low_out)
            at = pl.ds(pl.multiple_of(row + 8 * (1 - low_out), 8), 8)
            out_ref[slot_out, at, :] = out_ref[slot_out, at, :] + jnp.where(
                mask, pltpu.roll(piece, shift, 1), 0.0
            )

        correct(now.sub_slot, then.lr, then.dom_slot, now.ls)
        correct(now.dom_slot, then.ls, then.sub_slot, now.lr)


def coefficients():
    centre = 0.5 * (cheb_high + cheb_low)
    half_width = 0.5 * (cheb_high - cheb_low)
    ratio = centre / half_width
    rho_now = 1.0 / ratio
    steps = []
    for step in range(APPLY):
        rho_new = 1.0 / (2.0 * ratio - rho_now)
        steps.append((rho_new * rho_now, 2.0 * rho_new / half_width))
        rho_now = rho_new
    return centre, steps


def first_kernel(sizes, centre, parts_ref, recv_ref, recv2_ref, geo_ref, table_ref, residual_ref, diag_ref, direction_ref, image_ref, send_ref, later_ref, work_ref):
    sides = (Side(sizes, 0), Side(sizes, 1))
    residual_ref[...] = parts_ref[0]
    diag_ref[...] = parts_ref[1]
    for field, ref in ((0, residual_ref), (1, diag_ref)):
        add_faces(ref, recv_ref, field, sides[0])
        add_faces(ref, recv2_ref, field, sides[1])
    direction_ref[...] = residual_ref[...] / diag_ref[...] / centre
    apply_operator(direction_ref, geo_ref, table_ref, image_ref, work_ref)
    join_local(image_ref)
    emit_faces(image_ref, 0, send_ref, later_ref, sides)


def step_kernel(sizes, pair, part_ref, recv_ref, recv2_ref, geo_ref, table_ref, old_residual_ref, diag_ref, old_direction_ref, residual_ref, direction_ref, image_ref, send_ref, later_ref, work_ref):
    sides = (Side(sizes, 0), Side(sizes, 1))
    work_ref[...] = part_ref[...]
    add_faces(work_ref, recv_ref, 0, sides[0])
    add_faces(work_ref, recv2_ref, 0, sides[1])
    residual = old_residual_ref[...] - work_ref[...]
    residual_ref[...] = residual
    direction_ref[...] = pair[0] * old_direction_ref[...] + pair[1] * (residual / diag_ref[...])
    apply_operator(direction_ref, geo_ref, table_ref, image_ref, work_ref)
    join_local(image_ref)
    emit_faces(image_ref, 0, send_ref, later_ref, sides)


def end_kernel(sizes, pair, part_ref, recv_ref, recv2_ref, residual_ref, diag_ref, d0_ref, d1_ref, d2_ref, d3_ref, cells_ref, out_ref, work_ref):
    sides = (Side(sizes, 0), Side(sizes, 1))
    work_ref[...] = part_ref[...]
    add_faces(work_ref, recv_ref, 0, sides[0])
    add_faces(work_ref, recv2_ref, 0, sides[1])
    cell = lax.broadcasted_iota(jnp.int32, (LANES, LANES), 0)
    by_cell = jnp.where(cell == jnp.broadcast_to(cells_ref[...], (LANES, LANES)), 1.0, 0.0)
    table = by_cell.astype(jnp.bfloat16)
    for i in range(NP):
        at = slice(i * 64, i * 64 + 64)
        residual = residual_ref[at, :] - work_ref[at, :]
        last = d3_ref[at, :]
        direction = pair[0] * last + pair[1] * (residual / diag_ref[at, :])
        iterate = d0_ref[at, :] + d1_ref[at, :] + d2_ref[at, :] + last + direction
        out_ref[at, :] = permute_exact(iterate, table)


def call(kernel, outs, *operands, scratch=True, name=None):
    return pl.pallas_call(
        kernel,
        out_shape=outs,
        scratch_shapes=[pltpu.VMEM((ROWS, LANES), jnp.float32)] if scratch else [],
        compiler_params=pltpu.CompilerParams(vmem_limit_bytes=32 * 2**20),
        name=name,
    )(*operands)


def exchange_groups(sizes, stage):
    dom, sub = sizes
    groups = []
    for a in range(stage, dom + stage, 2):
        for b in range(stage, sub + stage, 2):
            groups.append(
                [((a + da) % dom) * sub + (b + db) % sub for da in (0, 1) for db in (0, 1)]
            )
    return groups


def solution(mesh):
    sizes = (mesh.shape["dom"], mesh.shape["sub"])
    apply_table, diag_table, middle = tables()
    middle = [float(value) for value in middle]
    centre, steps = coefficients()
    field = jax.ShapeDtypeStruct((ROWS, LANES), jnp.float32)
    one = jax.ShapeDtypeStruct((4, 16, LANES), jnp.float32)
    two = jax.ShapeDtypeStruct((4, 32, LANES), jnp.float32)

    def exchange(send, stage):
        return lax.all_to_all(
            send,
            ("dom", "sub"),
            0,
            0,
            axis_index_groups=exchange_groups(sizes, stage),
            tiled=True,
        )

    def assemble(send, later, fields):
        shape = one if fields == 1 else two
        recv = exchange(send, 0)
        send2 = call(
            functools.partial(middle_kernel, sizes, fields), shape, recv, later, scratch=False, name="faces"
        )
        return recv, exchange(send2, 1)

    def shards(geometry, load, cells):
        table = jnp.asarray(apply_table)
        geo, parts, send, later = call(
            functools.partial(begin_kernel, sizes, middle),
            (
                jax.ShapeDtypeStruct(geometry.shape, jnp.bfloat16),
                jax.ShapeDtypeStruct((2, ROWS, LANES), jnp.float32),
                two,
                two,
            ),
            geometry,
            load,
            cells,
            jnp.asarray(diag_table),
            name="begin",
        )
        recv, recv2 = assemble(send, later, 2)
        residual, diag, direction, image, send, later = call(
            functools.partial(first_kernel, sizes, centre),
            (field, field, field, field, one, one),
            parts,
            recv,
            recv2,
            geo,
            table,
            name="first",
        )
        directions = [direction]
        for pair in steps[:-1]:
            recv, recv2 = assemble(send, later, 1)
            residual, direction, image, send, later = call(
                functools.partial(step_kernel, sizes, pair),
                (field, field, field, one, one),
                image,
                recv,
                recv2,
                geo,
                table,
                residual,
                diag,
                direction,
                name="step",
            )
            directions.append(direction)
        recv, recv2 = assemble(send, later, 1)
        return call(
            functools.partial(end_kernel, sizes, steps[-1]),
            field,
            image,
            recv,
            recv2,
            residual,
            diag,
            *directions,
            cells,
            name="end",
        )

    placed = (P(None, None, ("dom", "sub")), P(None, ("dom", "sub")), P(("dom", "sub"), None))
    return jax.shard_map(
        shards, mesh=mesh, in_specs=placed, out_specs=P(None, ("dom", "sub")), check_vma=False
    )
```

profile of v0, /device:TPU:31, one launch (start us, length us, event | category | flops | bytes accessed | tf_op | source)
XLA Modules:
  0.0 113.8 jit_solution(464722280148783447)
XLA Ops:
  0.0 0.0 copy-start.1
  0.0 1.1 copy-done.1
  1.1 0.0 copy-start.2
  1.1 0.9 copy-done.2
  2.1 0.0 copy-start.3
  2.1 0.8 copy-done.3
  2.9 0.0 copy-start.4
  2.9 0.7 copy-done.4
  3.6 1.4 %begin.1 = (bf16[6,512,128]{2,1,0:T(8,128)(2,1)S(1)}, f32[2,512,128]{2,1,0:T(8,128)S(1)}, f32[4,32,128]{2,1,0:T(8,128)S(1)}, f32[4,32,128]{2,1,0:T(8,128)S(1)}) custom-call(bf16[6,512,128]{2,1,0:T(8,128)(2,1)S(1)} %copy-done.1, f32[512,128]{1,0:T(8,128)S(1)} %copy-done.2, s32[1,128]{1,0:T(1,128)S(1)} %copy-done.4, bf16[128,192]{1,0:T(8,128)(2,1)S(1)} %copy-done.3), custom_call_target="tpu_custom_call" | custom-call | tf_op jit(solution)/shard_map/begin/pallas_call | solution.py:366
  4.9 7.4 %all_to_all.50.recv_ref = f32[4,32,128]{2,1,0:T(8,128)S(1)} all-to-all(f32[4,32,128]{2,1,0:T(8,128)S(1)} %get-tuple-element.31), channel_id=1, replica_groups={{0,1,12,13},{2,3,14,15},{4,5,16,17},{6,7,18,19},{8,9,20,21},{10,11,22,2..., dimensions={0} | all-to-all | bytes 131072 | tf_op jit(solution)/shard_map/all_to_all | solution.py:396
  12.3 0.0 copy-start
  12.3 0.1 faces.5
  12.4 20.8 %all_to_all.51.recv2_ref = f32[4,32,128]{2,1,0:T(8,128)S(1)} all-to-all(f32[4,32,128]{2,1,0:T(8,128)S(1)} %faces.5), channel_id=1, replica_groups={{13,14,25,26},{15,16,27,28},{17,18,29,30},{19,20,31,32},{21,22,33,34},{..., dimensions={0} | all-to-all | bytes 131072 | tf_op jit(solution)/shard_map/all_to_all | solution.py:396
  33.3 0.0 copy-done
  33.3 2.4 %first.1 = (f32[512,128]{1,0:T(8,128)S(1)}, f32[512,128]{1,0:T(8,128)S(1)}, f32[512,128]{1,0:T(8,128)S(1)}, f32[512,128]{1,0:T(8,128)S(1)}, f32[4,16,128]{2,1,0:T(8,128)S(1)}, /*index=5*/f32[4,16,128]{2,1,0:T(8,128)S(1)}) custom-call(f32[2,512,128]{2,1,0:T(8,128)S(1)} %get-tuple-element.30.parts_ref, f32[4,32,128]{2,1,0:T(8,128)S(1)} %all_to_all.50.recv_ref, ...), custom_call_target="tpu_custom_call" | custom-call | tf_op jit(solution)/shard_map/first/pallas_call | solution.py:366
  35.7 4.7 %all_to_all.52.recv_ref = f32[4,16,128]{2,1,0:T(8,128)S(1)} all-to-all(f32[4,16,128]{2,1,0:T(8,128)S(1)} %get-tuple-element.35), channel_id=1, replica_groups={{0,1,12,13},{2,3,14,15},{4,5,16,17},{6,7,18,19},{8,9,20,21},{10,11,22,2..., dimensions={0} | all-to-all | bytes 65536 | tf_op jit(solution)/shard_map/all_to_all | solution.py:396
  40.4 0.1 faces.6
  40.5 12.1 %all_to_all.53.recv2_ref = f32[4,16,128]{2,1,0:T(8,128)S(1)} all-to-all(f32[4,16,128]{2,1,0:T(8,128)S(1)} %faces.6), channel_id=1, replica_groups={{13,14,25,26},{15,16,27,28},{17,18,29,30},{19,20,31,32},{21,22,33,34},{..., dimensions={0} | all-to-all | bytes 65536 | tf_op jit(solution)/shard_map/all_to_all | solution.py:396
  52.6 2.4 %step.3 = (f32[512,128]{1,0:T(8,128)S(1)}, f32[512,128]{1,0:T(8,128)S(1)}, f32[512,128]{1,0:T(8,128)S(1)}, f32[4,16,128]{2,1,0:T(8,128)S(1)}, f32[4,16,128]{2,1,0:T(8,128)S(1)}) custom-call(f32[512,128]{1,0:T(8,128)S(1)} %get-tuple-element.34.part_ref, f32[4,16,128]{2,1,0:T(8,128)S(1)} %all_to_all.52.recv_ref, f32[4,16,128]{2,1,0:T(8,128)S(1)} %all_to_all.53.recv2_ref, ...), custom_call_target="tpu_custom_call" | custom-call | tf_op jit(solution)/shard_map/step/pallas_call | solution.py:366
  55.0 4.7 %all_to_all.54.recv_ref = f32[4,16,128]{2,1,0:T(8,128)S(1)} all-to-all(f32[4,16,128]{2,1,0:T(8,128)S(1)} %get-tuple-element.41), channel_id=1, replica_groups={{0,1,12,13},{2,3,14,15},{4,5,16,17},{6,7,18,19},{8,9,20,21},{10,11,22,2..., dimensions={0} | all-to-all | bytes 65536 | tf_op jit(solution)/shard_map/all_to_all | solution.py:396
  59.8 0.1 faces.7
  59.8 12.2 %all_to_all.55.recv2_ref = f32[4,16,128]{2,1,0:T(8,128)S(1)} all-to-all(f32[4,16,128]{2,1,0:T(8,128)S(1)} %faces.7), channel_id=1, replica_groups={{13,14,25,26},{15,16,27,28},{17,18,29,30},{19,20,31,32},{21,22,33,34},{..., dimensions={0} | all-to-all | bytes 65536 | tf_op jit(solution)/shard_map/all_to_all | solution.py:396
  72.0 2.4 %step.4 = (f32[512,128]{1,0:T(8,128)S(1)}, f32[512,128]{1,0:T(8,128)S(1)}, f32[512,128]{1,0:T(8,128)S(1)}, f32[4,16,128]{2,1,0:T(8,128)S(1)}, f32[4,16,128]{2,1,0:T(8,128)S(1)}) custom-call(f32[512,128]{1,0:T(8,128)S(1)} %get-tuple-element.40.part_ref, f32[4,16,128]{2,1,0:T(8,128)S(1)} %all_to_all.54.recv_ref, f32[4,16,128]{2,1,0:T(8,128)S(1)} %all_to_all.55.recv2_ref, ...), custom_call_target="tpu_custom_call" | custom-call | tf_op jit(solution)/shard_map/step/pallas_call | solution.py:366
  74.4 5.4 %all_to_all.56.recv_ref = f32[4,16,128]{2,1,0:T(8,128)S(1)} all-to-all(f32[4,16,128]{2,1,0:T(8,128)S(1)} %get-tuple-element.46), channel_id=1, replica_groups={{0,1,12,13},{2,3,14,15},{4,5,16,17},{6,7,18,19},{8,9,20,21},{10,11,22,2..., dimensions={0} | all-to-all | bytes 65536 | tf_op jit(solution)/shard_map/all_to_all | solution.py:396
  79.8 0.1 faces.8
  79.9 11.5 %all_to_all.57.recv2_ref = f32[4,16,128]{2,1,0:T(8,128)S(1)} all-to-all(f32[4,16,128]{2,1,0:T(8,128)S(1)} %faces.8), channel_id=1, replica_groups={{13,14,25,26},{15,16,27,28},{17,18,29,30},{19,20,31,32},{21,22,33,34},{..., dimensions={0} | all-to-all | bytes 65536 | tf_op jit(solution)/shard_map/all_to_all | solution.py:396
  91.4 2.4 %step.5 = (f32[512,128]{1,0:T(8,128)S(1)}, f32[512,128]{1,0:T(8,128)S(1)}, f32[512,128]{1,0:T(8,128)S(1)}, f32[4,16,128]{2,1,0:T(8,128)S(1)}, f32[4,16,128]{2,1,0:T(8,128)S(1)}) custom-call(f32[512,128]{1,0:T(8,128)S(1)} %get-tuple-element.45.part_ref, f32[4,16,128]{2,1,0:T(8,128)S(1)} %all_to_all.56.recv_ref, f32[4,16,128]{2,1,0:T(8,128)S(1)} %all_to_all.57.recv2_ref, ...), custom_call_target="tpu_custom_call" | custom-call | tf_op jit(solution)/shard_map/step/pallas_call | solution.py:366
  93.9 6.6 %all_to_all.58.recv_ref = f32[4,16,128]{2,1,0:T(8,128)S(1)} all-to-all(f32[4,16,128]{2,1,0:T(8,128)S(1)} %get-tuple-element.51), channel_id=1, replica_groups={{0,1,12,13},{2,3,14,15},{4,5,16,17},{6,7,18,19},{8,9,20,21},{10,11,22,2..., dimensions={0} | all-to-all | bytes 65536 | tf_op jit(solution)/shard_map/all_to_all | solution.py:396
  100.4 0.1 faces.9
  100.5 11.5 %all_to_all.59.recv2_ref = f32[4,16,128]{2,1,0:T(8,128)S(1)} all-to-all(f32[4,16,128]{2,1,0:T(8,128)S(1)} %faces.9), channel_id=1, replica_groups={{13,14,25,26},{15,16,27,28},{17,18,29,30},{19,20,31,32},{21,22,33,34},{..., dimensions={0} | all-to-all | bytes 65536 | tf_op jit(solution)/shard_map/all_to_all | solution.py:396
  112.0 0.7 copy-done.5
  112.6 1.2 %end.1 = f32[512,128]{1,0:T(8,128)} custom-call(f32[512,128]{1,0:T(8,128)S(1)} %get-tuple-element.50.part_ref, f32[4,16,128]{2,1,0:T(8,128)S(1)} %all_to_all.58.recv_ref, f32[4,16,128]{2,1,0:T(8,128)S(1)} %all_to_all.59.recv2_ref, f32[512,128]{1,0:T(8,128)S(1)} %get-tuple-element.53.residual_ref, f32[512,128]{1,0:T(8,128)S(1)} %get-tuple-element.38.diag_ref, ...), custom_call_target="tpu_custom_call" | custom-call | tf_op jit(solution)/shard_map/end/pallas_call | solution.py:366
  (1 shorter events, 0.0 us)
Async XLA Ops:
  0.0 1.1 copy-start.1
  1.1 0.9 copy-start.2
  2.1 0.8 copy-start.3
  2.9 0.7 copy-start.4
  12.3 20.9 %copy-start = (bf16[256,192]{1,0:T(8,128)(2,1)S(1)}, bf16[256,192]{1,0:T(8,128)(2,1)}, u32[]{:S(2)}) copy-start(bf16[256,192]{1,0:T(8,128)(2,1)} %constant.4.clone.table_ref) | copy-start | bytes 294916
  112.0 0.7 copy-start.5
where the time goes:
time: 114 us
  blocking collectives  96.9 us (85%)
  Pallas kernels  12.6 us (11%)
  local copies, waits for them, and re-layouts  4.23 us (4%)
    all_to_all x10, blocking collectives, exchange(): lax.all_to_all(send, ('dom', 'sub'), 0, 0, axis_index_groups=exchange_gro...  96.9 us
    pallas_call x11, Pallas kernels, call(): pl.pallas_call(kernel, out_shape=outs, scratch_shapes=[pltpu.VMEM((ROWS,...  12.6 us
    unnamed x12, local copies, waits for them, and re-layouts  4.23 us

commit v1 on v0

--- a/solution.py
+++ b/solution.py
@@ -11,6 +11,7 @@
 
 NP = 8
 APPLY = 4
+ORDERS = ((0, 1),) * 5
 LANES = 128
 ROWS = NP**3
 
@@ -61,16 +62,13 @@
 def tables():
     derivative = derivative_table(NP).astype(np.float32).astype(np.float64)
     eye = np.eye(NP)
-    outer = three_products(np.kron(derivative, eye))
     inner = three_products(np.kron(eye, derivative))
-    outer_t = three_products(np.kron(derivative.T, eye))
     inner_t = three_products(np.kron(eye, derivative.T))
-    apply_table = np.concatenate([outer, inner, outer_t, inner_t], axis=0)
+    apply_table = np.concatenate([inner, inner_t], axis=0)
     square = derivative * derivative
-    diag_table = np.concatenate(
-        [three_products(np.kron(square.T, eye)), three_products(np.kron(eye, square.T))], axis=0
-    )
-    return apply_table, diag_table, np.diagonal(derivative)
+    diag_table = three_products(np.kron(eye, square.T))
+    rows = [[float(v) for v in row] for row in square.T]
+    return apply_table, diag_table, rows, [float(v) for v in np.diagonal(derivative)]
 
 
 def split_rows(values):
@@ -81,10 +79,6 @@
 
 def multiply(left, right):
     return jnp.dot(left, right, preferred_element_type=jnp.float32)
-
-
-def gather_first(ref, j):
-    return jnp.concatenate([ref[i * 64 + j * 8 : i * 64 + j * 8 + 8, :] for i in range(NP)], axis=0)
 
 
 def lane_of(rows):
@@ -116,20 +110,31 @@
 
 
 class Side:
-    def __init__(self, sizes, stage):
+    def __init__(self, sizes, parity):
         a = lax.axis_index("dom")
         b = lax.axis_index("sub")
-        self.lr = lax.rem(a + stage, 2)
-        self.ls = lax.rem(b + stage, 2)
-        self.place = 2 * self.lr + self.ls
-        self.dom_slot = 2 * (1 - self.lr) + self.ls
-        self.sub_slot = 2 * self.lr + (1 - self.ls)
-        self.far_slot = 3 - self.place
+        last_a = sizes[0] - 1
+        last_b = sizes[1] - 1
+        self.lr = lax.rem(a + parity, 2)
+        self.ls = lax.rem(b + parity, 2)
         self.vr = None
         self.vs = None
-        if stage:
-            self.vr = jnp.where(self.lr == 1, a > 0, a < sizes[0] - 1)
-            self.vs = jnp.where(self.ls == 1, b > 0, b < sizes[1] - 1)
+        place = 2 * self.lr + self.ls
+        dom_step, sub_step = 2, 1
+        if parity:
+            self.vr = jnp.where(self.lr == 1, a > 0, a < last_a)
+            self.vs = jnp.where(self.ls == 1, b > 0, b < last_b)
+            row = jnp.logical_or(b == 0, b == last_b)
+            column = jnp.logical_or(a == 0, a == last_a)
+            rest = jnp.logical_and(a == last_a, b > last_b - 3)
+            in_column = ((b + 3) & 3) + jnp.where(rest, 2, 0)
+            place = jnp.where(row, (a + 1) & 3, jnp.where(column, in_column, place))
+            dom_step = jnp.where(row, 1, 2)
+            sub_step = jnp.where(row, 2, 1)
+        self.place = place
+        self.dom_slot = place ^ dom_step
+        self.sub_slot = place ^ sub_step
+        self.far_slot = 3 - place
         self.i_row = pl.multiple_of((1 - self.lr) * 448, 64)
         self.j_row = (1 - self.ls) * 56
 
@@ -199,33 +204,71 @@
     ref[at, :] = ref[at, :] + jnp.where(mask, pltpu.roll(corner, shift, 1), 0.0)
 
 
+def halves(matrix):
+    flipped = matrix[:, ::-1]
+    even = 0.5 * (matrix + flipped)[:4, :4]
+    odd = 0.5 * (matrix - flipped)[:4, :4]
+    return [[float(v) for v in row] for row in even], [[float(v) for v in row] for row in odd]
+
+
+def blend(parts, matrix):
+    out = []
+    for row in matrix:
+        total = parts[0] * row[0]
+        for a in range(1, NP):
+            total = total + parts[a] * row[a]
+        out.append(total)
+    return out
+
+
+def derive(parts, pair):
+    even, odd = pair
+    sums = [parts[a] + parts[7 - a] for a in range(4)]
+    gaps = [parts[a] - parts[7 - a] for a in range(4)]
+    low = []
+    high = []
+    for i in range(4):
+        first = sums[0] * even[i][0]
+        second = gaps[0] * odd[i][0]
+        for a in range(1, 4):
+            first = first + sums[a] * even[i][a]
+            second = second + gaps[a] * odd[i][a]
+        low.append(second + first)
+        high.append(second - first)
+    return low + high[::-1]
+
+
 def apply_operator(value_ref, geo_ref, table_ref, image_ref, work_ref):
-    outer = table_ref[0:64, :]
-    both = table_ref[0:128, :]
-    outer_t = table_ref[128:192, :]
-    inner_t = table_ref[192:256, :]
+    forward, backward = PAIRS
+    inner = table_ref[0:64, :]
+    inner_t = table_ref[64:128, :]
     for j in range(NP):
-        product = multiply(outer, split_rows(gather_first(value_ref, j)))
-        for i in range(NP):
-            work_ref[i * 64 + j * 8 : i * 64 + j * 8 + 8, :] = product[i * 8 : i * 8 + 8, :]
+        rows = [slice(i * 64 + j * 8, i * 64 + j * 8 + 8) for i in range(NP)]
+        for at, part in zip(rows, derive([value_ref[at, :] for at in rows], forward)):
+            work_ref[at, :] = part
     for i in range(NP):
         at = slice(i * 64, i * 64 + 64)
-        product = multiply(both, split_rows(value_ref[at, :]))
+        rows = [slice(i * 64 + j * 8, i * 64 + j * 8 + 8) for j in range(NP)]
+        grad_t = multiply(inner, split_rows(value_ref[at, :]))
         grad_r = work_ref[at, :]
-        grad_s = product[0:64, :]
-        grad_t = product[64:128, :]
+        grad_s = jnp.concatenate(derive([value_ref[row, :] for row in rows], forward), axis=0)
         g = [geo_ref[index, at, :].astype(jnp.float32) for index in range(6)]
         work_ref[at, :] = g[0] * grad_r + g[3] * grad_s + g[4] * grad_t
         flux_s = g[3] * grad_r + g[1] * grad_s + g[5] * grad_t
         flux_t = g[4] * grad_r + g[5] * grad_s + g[2] * grad_t
-        image_ref[at, :] = multiply(outer_t, split_rows(flux_s)) + multiply(
+        from_s = derive([flux_s[j * 8 : j * 8 + 8, :] for j in range(NP)], backward)
+        image_ref[at, :] = jnp.concatenate(from_s, axis=0) + multiply(
             inner_t, split_rows(flux_t)
         )
     for j in range(NP):
-        product = multiply(outer_t, split_rows(gather_first(work_ref, j)))
-        for i in range(NP):
-            at = slice(i * 64 + j * 8, i * 64 + j * 8 + 8)
-            image_ref[at, :] = image_ref[at, :] + product[i * 8 : i * 8 + 8, :]
+        rows = [slice(i * 64 + j * 8, i * 64 + j * 8 + 8) for i in range(NP)]
+        for at, part in zip(rows, derive([work_ref[at, :] for at in rows], backward)):
+            image_ref[at, :] = image_ref[at, :] + part
+
+
+PAIRS = tuple(
+    halves(m) for m in (derivative_table(NP).astype(np.float32), derivative_table(NP).T.astype(np.float32))
+)
 
 
 def emit_faces(ref, field, send_ref, later_ref, sides):
@@ -243,67 +286,84 @@
     return total
 
 
-def begin_kernel(sizes, middle, geo_ref, load_ref, cells_ref, table_ref, geo_out, parts_ref, send_ref, later_ref, work_ref):
-    listed = cells_ref[...]
+def begin_kernel(sizes, order, square, middle, geo_hbm, load_hbm, cells_hbm, table_hbm, geo_out, parts_ref, one_hot_ref, send_ref, later_ref, work_ref, geo_ref, load_ref, cells_ref, table_ref, sems):
+    copies = [pltpu.make_async_copy(cells_hbm, cells_ref, sems.at[0])]
+    for index in range(6):
+        copies.append(
+            pltpu.make_async_copy(geo_hbm.at[index], geo_ref.at[index], sems.at[1 + index])
+        )
+    copies.append(pltpu.make_async_copy(table_hbm, table_ref, sems.at[7]))
+    copies.append(pltpu.make_async_copy(load_hbm, load_ref, sems.at[8]))
+    for copy in copies:
+        copy.start()
+    copies[0].wait()
     cell = lax.broadcasted_iota(jnp.int32, (LANES, LANES), 0)
-    by_cell = jnp.where(cell == jnp.broadcast_to(listed, (LANES, LANES)), 1.0, 0.0)
+    by_cell = jnp.where(cell == jnp.broadcast_to(cells_ref[...], (LANES, LANES)), 1.0, 0.0)
+    one_hot_ref[...] = by_cell.astype(jnp.bfloat16)
     table = by_cell.T.astype(jnp.bfloat16)
-    for index in range(6):
-        geo_out[index] = multiply(geo_ref[index], table).astype(jnp.bfloat16)
-    outer = table_ref[0:64, :]
-    inner = table_ref[64:128, :]
-    work_ref[...] = geo_out[0].astype(jnp.float32)
     load_part = parts_ref.at[0]
     diag_part = parts_ref.at[1]
+    copies[1].wait()
+    first = multiply(geo_ref[0], table)
+    geo_out[0] = first.astype(jnp.bfloat16)
+    work_ref[...] = first
+    for index in range(1, 6):
+        copies[1 + index].wait()
+        geo_out[index] = multiply(geo_ref[index], table).astype(jnp.bfloat16)
+    copies[7].wait()
+    inner = table_ref[...]
+    for j in range(NP):
+        rows = [slice(i * 64 + j * 8, i * 64 + j * 8 + 8) for i in range(NP)]
+        for at, part in zip(rows, blend([work_ref[at, :] for at in rows], square)):
+            diag_part[at, :] = part
+    copies[8].wait()
     sub_row = lax.broadcasted_iota(jnp.int32, (64, LANES), 0) % 8
     third = jnp.where(sub_row == 0, middle[0], jnp.where(sub_row == 7, middle[7], 0.0))
     for i in range(NP):
         at = slice(i * 64, i * 64 + 64)
         load_part[at, :] = permute_exact(load_ref[at, :], table)
-        first = split_rows(geo_out[1, at, :].astype(jnp.float32))
-        second = split_rows(geo_out[2, at, :].astype(jnp.float32))
-        total = multiply(outer, first) + multiply(inner, second)
-        if i in (0, 7):
-            total = total + 2.0 * middle[i] * third * geo_out[4, at, :].astype(jnp.float32)
-        diag_part[at, :] = total
+        second = geo_out[1, at, :].astype(jnp.float32)
+        fifth = geo_out[5, at, :].astype(jnp.float32)
+        pieces = blend([second[j * 8 : j * 8 + 8, :] for j in range(NP)], square)
         for j in (0, 7):
-            here = slice(i * 64 + j * 8, i * 64 + j * 8 + 8)
-            fifth = geo_out[5, at, :].astype(jnp.float32)[j * 8 : j * 8 + 8, :]
-            extra = middle[j] * third[0:8, :] * fifth
+            extra = middle[j] * third[0:8, :] * fifth[j * 8 : j * 8 + 8, :]
             if i in (0, 7):
                 cross = geo_out[3, at, :].astype(jnp.float32)[j * 8 : j * 8 + 8, :]
                 extra = extra + middle[i] * middle[j] * cross
-            diag_part[here, :] = diag_part[here, :] + 2.0 * extra
-    for j in range(NP):
-        product = multiply(outer, split_rows(gather_first(work_ref, j)))
-        for i in range(NP):
-            at = slice(i * 64 + j * 8, i * 64 + j * 8 + 8)
-            diag_part[at, :] = diag_part[at, :] + product[i * 8 : i * 8 + 8, :]
-    sides = (Side(sizes, 0), Side(sizes, 1))
+            pieces[j] = pieces[j] + 2.0 * extra
+        total = jnp.concatenate(pieces, axis=0)
+        total = total + multiply(inner, split_rows(geo_out[2, at, :].astype(jnp.float32)))
+        if i in (0, 7):
+            total = total + 2.0 * middle[i] * third * geo_out[4, at, :].astype(jnp.float32)
+        diag_part[at, :] = diag_part[at, :] + total
+    sides = two_sides(sizes, order)
     for field in range(2):
         join_local(parts_ref.at[field])
         emit_faces(parts_ref.at[field], field, send_ref, later_ref, sides)
 
 
-def middle_kernel(sizes, fields, recv_ref, later_ref, out_ref):
-    now = Side(sizes, 0)
-    then = Side(sizes, 1)
+def middle_kernel(sizes, order, fields, recv_ref, later_ref, out_ref):
+    now, then = two_sides(sizes, order)
     out_ref[...] = later_ref[...]
     lane = lane_of(8)
     for field in range(fields):
         row = field * 16
 
-        def correct(slot_in, low_in, slot_out, low_out):
+        def correct(slot_in, low_in, slot_out, low_out, valid):
             piece = recv_ref[slot_in, pl.ds(pl.multiple_of(row + 8 * (1 - low_in), 8), 8), :]
             shift = (8 + 128 - 8 * (1 - low_out) + 8 * (1 - low_in) - 8) & 127
-            mask = lane // 8 == 15 * (1 - low_out)
+            mask = keep(lane // 8 == 15 * (1 - low_out), valid)
             at = pl.ds(pl.multiple_of(row + 8 * (1 - low_out), 8), 8)
             out_ref[slot_out, at, :] = out_ref[slot_out, at, :] + jnp.where(
                 mask, pltpu.roll(piece, shift, 1), 0.0
             )
 
-        correct(now.sub_slot, then.lr, then.dom_slot, now.ls)
-        correct(now.dom_slot, then.ls, then.sub_slot, now.lr)
+        correct(now.sub_slot, then.lr, then.dom_slot, now.ls, now.vs)
+        correct(now.dom_slot, then.ls, then.sub_slot, now.lr, now.vr)
+
+
+def two_sides(sizes, order):
+    return Side(sizes, order[0]), Side(sizes, order[1])
 
 
 def coefficients():
@@ -319,8 +379,8 @@
     return centre, steps
 
 
-def first_kernel(sizes, centre, parts_ref, recv_ref, recv2_ref, geo_ref, table_ref, residual_ref, diag_ref, direction_ref, image_ref, send_ref, later_ref, work_ref):
-    sides = (Side(sizes, 0), Side(sizes, 1))
+def first_kernel(sizes, before, order, centre, parts_ref, recv_ref, recv2_ref, geo_ref, table_ref, residual_ref, diag_ref, direction_ref, image_ref, send_ref, later_ref, work_ref):
+    sides = two_sides(sizes, before)
     residual_ref[...] = parts_ref[0]
     diag_ref[...] = parts_ref[1]
     for field, ref in ((0, residual_ref), (1, diag_ref)):
@@ -329,11 +389,11 @@
     direction_ref[...] = residual_ref[...] / diag_ref[...] / centre
     apply_operator(direction_ref, geo_ref, table_ref, image_ref, work_ref)
     join_local(image_ref)
-    emit_faces(image_ref, 0, send_ref, later_ref, sides)
-
-
-def step_kernel(sizes, pair, part_ref, recv_ref, recv2_ref, geo_ref, table_ref, old_residual_ref, diag_ref, old_direction_ref, residual_ref, direction_ref, image_ref, send_ref, later_ref, work_ref):
-    sides = (Side(sizes, 0), Side(sizes, 1))
+    emit_faces(image_ref, 0, send_ref, later_ref, two_sides(sizes, order))
+
+
+def step_kernel(sizes, before, order, pair, part_ref, recv_ref, recv2_ref, geo_ref, table_ref, old_residual_ref, diag_ref, old_direction_ref, residual_ref, direction_ref, image_ref, send_ref, later_ref, work_ref):
+    sides = two_sides(sizes, before)
     work_ref[...] = part_ref[...]
     add_faces(work_ref, recv_ref, 0, sides[0])
     add_faces(work_ref, recv2_ref, 0, sides[1])
@@ -342,17 +402,16 @@
     direction_ref[...] = pair[0] * old_direction_ref[...] + pair[1] * (residual / diag_ref[...])
     apply_operator(direction_ref, geo_ref, table_ref, image_ref, work_ref)
     join_local(image_ref)
-    emit_faces(image_ref, 0, send_ref, later_ref, sides)
-
-
-def end_kernel(sizes, pair, part_ref, recv_ref, recv2_ref, residual_ref, diag_ref, d0_ref, d1_ref, d2_ref, d3_ref, cells_ref, out_ref, work_ref):
-    sides = (Side(sizes, 0), Side(sizes, 1))
+    emit_faces(image_ref, 0, send_ref, later_ref, two_sides(sizes, order))
+
+
+def end_kernel(sizes, before, pair, part_ref, recv_ref, recv2_ref, residual_ref, diag_ref, d0_ref, d1_ref, d2_ref, d3_ref, one_hot_ref, out_hbm, work_ref, out_ref, sems):
+    sides = two_sides(sizes, before)
     work_ref[...] = part_ref[...]
     add_faces(work_ref, recv_ref, 0, sides[0])
     add_faces(work_ref, recv2_ref, 0, sides[1])
-    cell = lax.broadcasted_iota(jnp.int32, (LANES, LANES), 0)
-    by_cell = jnp.where(cell == jnp.broadcast_to(cells_ref[...], (LANES, LANES)), 1.0, 0.0)
-    table = by_cell.astype(jnp.bfloat16)
+    table = one_hot_ref[...]
+    copies = []
     for i in range(NP):
         at = slice(i * 64, i * 64 + 64)
         residual = residual_ref[at, :] - work_ref[at, :]
@@ -360,88 +419,116 @@
         direction = pair[0] * last + pair[1] * (residual / diag_ref[at, :])
         iterate = d0_ref[at, :] + d1_ref[at, :] + d2_ref[at, :] + last + direction
         out_ref[at, :] = permute_exact(iterate, table)
-
-
-def call(kernel, outs, *operands, scratch=True, name=None):
+        if i % 2 == 1:
+            here = pl.ds((i - 1) * 64, 128)
+            copy = pltpu.make_async_copy(out_ref.at[here], out_hbm.at[here], sems.at[i // 2])
+            copy.start()
+            copies.append(copy)
+    for copy in copies:
+        copy.wait()
+
+
+def call(kernel, outs, *operands, scratch=(), name=None, **specs):
     return pl.pallas_call(
         kernel,
         out_shape=outs,
-        scratch_shapes=[pltpu.VMEM((ROWS, LANES), jnp.float32)] if scratch else [],
+        scratch_shapes=list(scratch),
         compiler_params=pltpu.CompilerParams(vmem_limit_bytes=32 * 2**20),
         name=name,
+        **specs,
     )(*operands)
 
 
-def exchange_groups(sizes, stage):
+def exchange_groups(sizes, parity):
     dom, sub = sizes
-    groups = []
-    for a in range(stage, dom + stage, 2):
-        for b in range(stage, sub + stage, 2):
-            groups.append(
-                [((a + da) % dom) * sub + (b + db) % sub for da in (0, 1) for db in (0, 1)]
-            )
-    return groups
+    whole = []
+    if parity:
+        for b in (0, sub - 1):
+            whole += [[((a + step) % dom, b) for step in range(4)] for a in range(-1, dom - 1, 4)]
+        full = 4 * ((sub - 2) // 4)
+        for a in (0, dom - 1):
+            whole += [[(a, b + step) for step in range(4)] for b in range(1, 1 + full, 4)]
+        whole.append([(a, b) for a in (0, dom - 1) for b in (sub - 3, sub - 2)])
+    for a in range(parity, dom - 1, 2):
+        for b in range(parity, sub - 1, 2):
+            whole.append([(a + da, b + db) for da in (0, 1) for db in (0, 1)])
+    return [[a * sub + b for a, b in group] for group in whole]
 
 
 def solution(mesh):
     sizes = (mesh.shape["dom"], mesh.shape["sub"])
-    apply_table, diag_table, middle = tables()
-    middle = [float(value) for value in middle]
+    apply_table, diag_table, square, middle = tables()
     centre, steps = coefficients()
     field = jax.ShapeDtypeStruct((ROWS, LANES), jnp.float32)
     one = jax.ShapeDtypeStruct((4, 16, LANES), jnp.float32)
     two = jax.ShapeDtypeStruct((4, 32, LANES), jnp.float32)
 
-    def exchange(send, stage):
+    work = pltpu.VMEM((ROWS, LANES), jnp.float32)
+    far = pl.BlockSpec(memory_space=pltpu.HBM)
+    near = pl.BlockSpec(memory_space=pltpu.VMEM)
+    orders = ORDERS
+
+    def exchange(send, parity):
         return lax.all_to_all(
             send,
             ("dom", "sub"),
             0,
             0,
-            axis_index_groups=exchange_groups(sizes, stage),
+            axis_index_groups=exchange_groups(sizes, parity),
             tiled=True,
         )
 
-    def assemble(send, later, fields):
+    def assemble(send, later, order, fields):
         shape = one if fields == 1 else two
-        recv = exchange(send, 0)
+        recv = exchange(send, order[0])
         send2 = call(
-            functools.partial(middle_kernel, sizes, fields), shape, recv, later, scratch=False, name="faces"
-        )
-        return recv, exchange(send2, 1)
+            functools.partial(middle_kernel, sizes, order, fields), shape, recv, later, name="faces"
+        )
+        return recv, exchange(send2, order[1])
 
     def shards(geometry, load, cells):
         table = jnp.asarray(apply_table)
-        geo, parts, send, later = call(
-            functools.partial(begin_kernel, sizes, middle),
+        geo, parts, one_hot, send, later = call(
+            functools.partial(begin_kernel, sizes, orders[0], square, middle),
             (
                 jax.ShapeDtypeStruct(geometry.shape, jnp.bfloat16),
                 jax.ShapeDtypeStruct((2, ROWS, LANES), jnp.float32),
+                jax.ShapeDtypeStruct((LANES, LANES), jnp.bfloat16),
                 two,
                 two,
             ),
-            geometry,
-            load,
-            cells,
-            jnp.asarray(diag_table),
+            *[
+                pltpu.with_memory_space_constraint(array, pltpu.HBM)
+                for array in (geometry, load, cells, jnp.asarray(diag_table))
+            ],
+            in_specs=[far] * 4,
+            scratch=(
+                work,
+                pltpu.VMEM(geometry.shape, jnp.bfloat16),
+                work,
+                pltpu.VMEM(cells.shape, jnp.int32),
+                pltpu.VMEM(diag_table.shape, jnp.bfloat16),
+                pltpu.SemaphoreType.DMA((9,)),
+            ),
             name="begin",
         )
-        recv, recv2 = assemble(send, later, 2)
+        recv, recv2 = assemble(send, later, orders[0], 2)
         residual, diag, direction, image, send, later = call(
-            functools.partial(first_kernel, sizes, centre),
+            functools.partial(first_kernel, sizes, orders[0], orders[1], centre),
             (field, field, field, field, one, one),
             parts,
             recv,
             recv2,
             geo,
             table,
+            scratch=(work,),
             name="first",
         )
         directions = [direction]
-        for pair in steps[:-1]:
-            recv, recv2 = assemble(send, later, 1)
+        for step, pair in enumerate(steps[:-1]):
+            recv, recv2 = assemble(send, later, orders[step + 1], 1)
             residual, direction, image, send, later = call(
-                functools.partial(step_kernel, sizes, pair),
+                functools.partial(step_kernel, sizes, orders[step + 1], orders[step + 2], pair),
                 (field, field, field, one, one),
                 image,
                 recv,
@@ -451,12 +538,13 @@
                 residual,
                 diag,
                 direction,
+                scratch=(work,),
                 name="step",
             )
             directions.append(direction)
-        recv, recv2 = assemble(send, later, 1)
+        recv, recv2 = assemble(send, later, orders[APPLY], 1)
         return call(
-            functools.partial(end_kernel, sizes, steps[-1]),
+            functools.partial(end_kernel, sizes, orders[APPLY], steps[-1]),
             field,
             image,
             recv,
@@ -464,7 +552,10 @@
             residual,
             diag,
             *directions,
-            cells,
+            one_hot,
+            in_specs=[near] * 10,
+            out_specs=far,
+            scratch=(work, work, pltpu.SemaphoreType.DMA((4,))),
             name="end",
         )
 

time: 114 us -> 106 us (0.930)
  the two profiles are of different devices: /device:TPU:31 before, /device:TPU:95 now
where the time goes in v1:
time: 106 us; the launch traced here: 105 us
  blocking collectives  95.8 us (90%)
  Pallas kernels  9.47 us (9%)
    all_to_all x10, blocking collectives, exchange(): lax.all_to_all(send, ('dom', 'sub'), 0, 0, axis_index_groups=exchange_gro...  95.8 us
    pallas_call x11, Pallas kernels, call(): pl.pallas_call(kernel, out_shape=outs, scratch_shapes=list(scratch), comp...  9.47 us

profile of v1, /device:TPU:95, one launch (start us, length us, event | category | flops | bytes accessed | tf_op | source)
XLA Modules:
  0.0 105.3 jit_solution(17707019448372443773)
XLA Ops:
  0.0 3.2 %begin.1 = (bf16[6,512,128]{2,1,0:T(8,128)(2,1)S(1)}, f32[2,512,128]{2,1,0:T(8,128)S(1)}, bf16[128,128]{1,0:T(8,128)(2,1)S(1)}, f32[4,32,128]{2,1,0:T(8,128)S(1)}, f32[4,32,128]{2,1,0:T(8,128)S(1)}) custom-call(bf16[6,512,128]{2,1,0:T(8,128)(2,1)} %geo_hbm.1, f32[512,128]{1,0:T(8,128)} %load_hbm.1, s32[1,128]{1,0:T(1,128)} %cells_hbm.1, ...), custom_call_target="tpu_custom_call" | custom-call | tf_op jit(solution)/shard_map/begin/pallas_call | solution.py:432
  3.3 5.5 %all_to_all.50.recv_ref = f32[4,32,128]{2,1,0:T(8,128)S(1)} all-to-all(f32[4,32,128]{2,1,0:T(8,128)S(1)} %get-tuple-element.32), channel_id=1, replica_groups={{0,1,12,13},{2,3,14,15},{4,5,16,17},{6,7,18,19},{8,9,20,21},{10,11,22,2..., dimensions={0} | all-to-all | bytes 131072 | tf_op jit(solution)/shard_map/all_to_all | solution.py:472
  8.7 0.1 faces.5
  8.8 0.0 copy-start
  8.8 15.7 %all_to_all.51.recv2_ref = f32[4,32,128]{2,1,0:T(8,128)S(1)} all-to-all(f32[4,32,128]{2,1,0:T(8,128)S(1)} %faces.5), channel_id=1, replica_groups={{756,0,12,24},{36,48,60,72},{84,96,108,120},{132,144,156,168},{180,192,..., dimensions={0} | all-to-all | bytes 131072 | tf_op jit(solution)/shard_map/all_to_all | solution.py:472
  24.5 0.0 copy-done
  24.5 1.2 %first.1 = (f32[512,128]{1,0:T(8,128)S(1)}, f32[512,128]{1,0:T(8,128)S(1)}, f32[512,128]{1,0:T(8,128)S(1)}, f32[512,128]{1,0:T(8,128)S(1)}, f32[4,16,128]{2,1,0:T(8,128)S(1)}, /*index=5*/f32[4,16,128]{2,1,0:T(8,128)S(1)}) custom-call(f32[2,512,128]{2,1,0:T(8,128)S(1)} %get-tuple-element.31.parts_ref, f32[4,32,128]{2,1,0:T(8,128)S(1)} %all_to_all.50.recv_ref, ...), custom_call_target="tpu_custom_call" | custom-call | tf_op jit(solution)/shard_map/first/pallas_call | solution.py:432
  25.7 4.7 %all_to_all.52.recv_ref = f32[4,16,128]{2,1,0:T(8,128)S(1)} all-to-all(f32[4,16,128]{2,1,0:T(8,128)S(1)} %get-tuple-element.36), channel_id=1, replica_groups={{0,1,12,13},{2,3,14,15},{4,5,16,17},{6,7,18,19},{8,9,20,21},{10,11,22,2..., dimensions={0} | all-to-all | bytes 65536 | tf_op jit(solution)/shard_map/all_to_all | solution.py:472
  30.4 0.1 faces.6
  30.4 16.6 %all_to_all.53.recv2_ref = f32[4,16,128]{2,1,0:T(8,128)S(1)} all-to-all(f32[4,16,128]{2,1,0:T(8,128)S(1)} %faces.6), channel_id=1, replica_groups={{756,0,12,24},{36,48,60,72},{84,96,108,120},{132,144,156,168},{180,192,..., dimensions={0} | all-to-all | bytes 65536 | tf_op jit(solution)/shard_map/all_to_all | solution.py:472
  47.0 1.2 %step.3 = (f32[512,128]{1,0:T(8,128)S(1)}, f32[512,128]{1,0:T(8,128)S(1)}, f32[512,128]{1,0:T(8,128)S(1)}, f32[4,16,128]{2,1,0:T(8,128)S(1)}, f32[4,16,128]{2,1,0:T(8,128)S(1)}) custom-call(f32[512,128]{1,0:T(8,128)S(1)} %get-tuple-element.35.part_ref, f32[4,16,128]{2,1,0:T(8,128)S(1)} %all_to_all.52.recv_ref, f32[4,16,128]{2,1,0:T(8,128)S(1)} %all_to_all.53.recv2_ref, ...), custom_call_target="tpu_custom_call" | custom-call | tf_op jit(solution)/shard_map/step/pallas_call | solution.py:432
  48.2 4.7 %all_to_all.54.recv_ref = f32[4,16,128]{2,1,0:T(8,128)S(1)} all-to-all(f32[4,16,128]{2,1,0:T(8,128)S(1)} %get-tuple-element.42), channel_id=1, replica_groups={{0,1,12,13},{2,3,14,15},{4,5,16,17},{6,7,18,19},{8,9,20,21},{10,11,22,2..., dimensions={0} | all-to-all | bytes 65536 | tf_op jit(solution)/shard_map/all_to_all | solution.py:472
  52.8 0.1 faces.7
  52.9 13.8 %all_to_all.55.recv2_ref = f32[4,16,128]{2,1,0:T(8,128)S(1)} all-to-all(f32[4,16,128]{2,1,0:T(8,128)S(1)} %faces.7), channel_id=1, replica_groups={{756,0,12,24},{36,48,60,72},{84,96,108,120},{132,144,156,168},{180,192,..., dimensions={0} | all-to-all | bytes 65536 | tf_op jit(solution)/shard_map/all_to_all | solution.py:472
  66.7 1.2 %step.4 = (f32[512,128]{1,0:T(8,128)S(1)}, f32[512,128]{1,0:T(8,128)S(1)}, f32[512,128]{1,0:T(8,128)S(1)}, f32[4,16,128]{2,1,0:T(8,128)S(1)}, f32[4,16,128]{2,1,0:T(8,128)S(1)}) custom-call(f32[512,128]{1,0:T(8,128)S(1)} %get-tuple-element.41.part_ref, f32[4,16,128]{2,1,0:T(8,128)S(1)} %all_to_all.54.recv_ref, f32[4,16,128]{2,1,0:T(8,128)S(1)} %all_to_all.55.recv2_ref, ...), custom_call_target="tpu_custom_call" | custom-call | tf_op jit(solution)/shard_map/step/pallas_call | solution.py:432
  67.8 4.7 %all_to_all.56.recv_ref = f32[4,16,128]{2,1,0:T(8,128)S(1)} all-to-all(f32[4,16,128]{2,1,0:T(8,128)S(1)} %get-tuple-element.47), channel_id=1, replica_groups={{0,1,12,13},{2,3,14,15},{4,5,16,17},{6,7,18,19},{8,9,20,21},{10,11,22,2..., dimensions={0} | all-to-all | bytes 65536 | tf_op jit(solution)/shard_map/all_to_all | solution.py:472
  72.5 0.1 faces.8
  72.6 13.5 %all_to_all.57.recv2_ref = f32[4,16,128]{2,1,0:T(8,128)S(1)} all-to-all(f32[4,16,128]{2,1,0:T(8,128)S(1)} %faces.8), channel_id=1, replica_groups={{756,0,12,24},{36,48,60,72},{84,96,108,120},{132,144,156,168},{180,192,..., dimensions={0} | all-to-all | bytes 65536 | tf_op jit(solution)/shard_map/all_to_all | solution.py:472
  86.0 1.2 %step.5 = (f32[512,128]{1,0:T(8,128)S(1)}, f32[512,128]{1,0:T(8,128)S(1)}, f32[512,128]{1,0:T(8,128)S(1)}, f32[4,16,128]{2,1,0:T(8,128)S(1)}, f32[4,16,128]{2,1,0:T(8,128)S(1)}) custom-call(f32[512,128]{1,0:T(8,128)S(1)} %get-tuple-element.46.part_ref, f32[4,16,128]{2,1,0:T(8,128)S(1)} %all_to_all.56.recv_ref, f32[4,16,128]{2,1,0:T(8,128)S(1)} %all_to_all.57.recv2_ref, ...), custom_call_target="tpu_custom_call" | custom-call | tf_op jit(solution)/shard_map/step/pallas_call | solution.py:432
  87.2 4.7 %all_to_all.58.recv_ref = f32[4,16,128]{2,1,0:T(8,128)S(1)} all-to-all(f32[4,16,128]{2,1,0:T(8,128)S(1)} %get-tuple-element.52), channel_id=1, replica_groups={{0,1,12,13},{2,3,14,15},{4,5,16,17},{6,7,18,19},{8,9,20,21},{10,11,22,2..., dimensions={0} | all-to-all | bytes 65536 | tf_op jit(solution)/shard_map/all_to_all | solution.py:472
  91.8 0.1 faces.9
  91.9 12.3 %all_to_all.59.recv2_ref = f32[4,16,128]{2,1,0:T(8,128)S(1)} all-to-all(f32[4,16,128]{2,1,0:T(8,128)S(1)} %faces.9), channel_id=1, replica_groups={{756,0,12,24},{36,48,60,72},{84,96,108,120},{132,144,156,168},{180,192,..., dimensions={0} | all-to-all | bytes 65536 | tf_op jit(solution)/shard_map/all_to_all | solution.py:472
  104.2 1.1 %end.1 = f32[512,128]{1,0:T(8,128)} custom-call(f32[512,128]{1,0:T(8,128)S(1)} %get-tuple-element.51.part_ref, f32[4,16,128]{2,1,0:T(8,128)S(1)} %all_to_all.58.recv_ref, f32[4,16,128]{2,1,0:T(8,128)S(1)} %all_to_all.59.recv2_ref, f32[512,128]{1,0:T(8,128)S(1)} %get-tuple-element.54.residual_ref, f32[512,128]{1,0:T(8,128)S(1)} %get-tuple-element.39.diag_ref, ...), custom_call_target="tpu_custom_call" | custom-call | tf_op jit(solution)/shard_map/end/pallas_call | solution.py:432
Async XLA Ops:
  8.8 15.7 %copy-start = (bf16[128,192]{1,0:T(8,128)(2,1)S(1)}, bf16[128,192]{1,0:T(8,128)(2,1)}, u32[]{:S(2)}) copy-start(bf16[128,192]{1,0:T(8,128)(2,1)} %constant.4.clone.table_ref) | copy-start | bytes 147460

commit v2 on v1

--- a/solution.py
+++ b/solution.py
@@ -11,7 +11,7 @@
 
 NP = 8
 APPLY = 4
-ORDERS = ((0, 1),) * 5
+ORDERS = ((0, 1), (1, 0), (0, 1), (1, 0), (0, 1))
 LANES = 128
 ROWS = NP**3
 
@@ -287,13 +287,17 @@
 
 
 def begin_kernel(sizes, order, square, middle, geo_hbm, load_hbm, cells_hbm, table_hbm, geo_out, parts_ref, one_hot_ref, send_ref, later_ref, work_ref, geo_ref, load_ref, cells_ref, table_ref, sems):
-    copies = [pltpu.make_async_copy(cells_hbm, cells_ref, sems.at[0])]
-    for index in range(6):
-        copies.append(
-            pltpu.make_async_copy(geo_hbm.at[index], geo_ref.at[index], sems.at[1 + index])
-        )
-    copies.append(pltpu.make_async_copy(table_hbm, table_ref, sems.at[7]))
-    copies.append(pltpu.make_async_copy(load_hbm, load_ref, sems.at[8]))
+    copies = [
+        pltpu.make_async_copy(source, target, sems.at[index])
+        for index, (source, target) in enumerate(
+            (
+                (cells_hbm, cells_ref),
+                (geo_hbm, geo_ref),
+                (load_hbm, load_ref),
+                (table_hbm, table_ref),
+            )
+        )
+    ]
     for copy in copies:
         copy.start()
     copies[0].wait()
@@ -303,20 +307,18 @@
     table = by_cell.T.astype(jnp.bfloat16)
     load_part = parts_ref.at[0]
     diag_part = parts_ref.at[1]
-    copies[1].wait()
-    first = multiply(geo_ref[0], table)
-    geo_out[0] = first.astype(jnp.bfloat16)
-    work_ref[...] = first
-    for index in range(1, 6):
-        copies[1 + index].wait()
-        geo_out[index] = multiply(geo_ref[index], table).astype(jnp.bfloat16)
-    copies[7].wait()
+    for copy in copies[1:]:
+        copy.wait()
+    for index in range(6):
+        moved = multiply(geo_ref[index], table)
+        geo_out[index] = moved.astype(jnp.bfloat16)
+        if index == 0:
+            work_ref[...] = moved
     inner = table_ref[...]
     for j in range(NP):
         rows = [slice(i * 64 + j * 8, i * 64 + j * 8 + 8) for i in range(NP)]
         for at, part in zip(rows, blend([work_ref[at, :] for at in rows], square)):
             diag_part[at, :] = part
-    copies[8].wait()
     sub_row = lax.broadcasted_iota(jnp.int32, (64, LANES), 0) % 8
     third = jnp.where(sub_row == 0, middle[0], jnp.where(sub_row == 7, middle[7], 0.0))
     for i in range(NP):
@@ -508,7 +510,7 @@
                 work,
                 pltpu.VMEM(cells.shape, jnp.int32),
                 pltpu.VMEM(diag_table.shape, jnp.bfloat16),
-                pltpu.SemaphoreType.DMA((9,)),
+                pltpu.SemaphoreType.DMA((4,)),
             ),
             name="begin",
         )

time: 106 us -> 104 us (0.981)
  the two profiles are of different devices: /device:TPU:95 before, /device:TPU:64 now
where the time goes in v2:
time: 104 us; the launch traced here: 103 us
  blocking collectives  94.7 us (91%)
  Pallas kernels  8.66 us (8%)
    all_to_all x10, blocking collectives, exchange(): lax.all_to_all(send, ('dom', 'sub'), 0, 0, axis_index_groups=exchange_gro...  94.7 us
    pallas_call x11, Pallas kernels, call(): pl.pallas_call(kernel, out_shape=outs, scratch_shapes=list(scratch), comp...  8.66 us

profile of v2, /device:TPU:64, one launch (start us, length us, event | category | flops | bytes accessed | tf_op | source)
XLA Modules:
  0.0 103.4 jit_solution(3464209782487013680)
XLA Ops:
  0.0 2.4 %begin.1 = (bf16[6,512,128]{2,1,0:T(8,128)(2,1)S(1)}, f32[2,512,128]{2,1,0:T(8,128)S(1)}, bf16[128,128]{1,0:T(8,128)(2,1)S(1)}, f32[4,32,128]{2,1,0:T(8,128)S(1)}, f32[4,32,128]{2,1,0:T(8,128)S(1)}) custom-call(bf16[6,512,128]{2,1,0:T(8,128)(2,1)} %geo_hbm.1, f32[512,128]{1,0:T(8,128)} %load_hbm.1, s32[1,128]{1,0:T(1,128)} %cells_hbm.1, ...), custom_call_target="tpu_custom_call" | custom-call | tf_op jit(solution)/shard_map/begin/pallas_call | solution.py:434
  2.4 13.1 %all_to_all.50.recv_ref = f32[4,32,128]{2,1,0:T(8,128)S(1)} all-to-all(f32[4,32,128]{2,1,0:T(8,128)S(1)} %get-tuple-element.32), channel_id=1, replica_groups={{0,1,12,13},{2,3,14,15},{4,5,16,17},{6,7,18,19},{8,9,20,21},{10,11,22,2..., dimensions={0} | all-to-all | bytes 131072 | tf_op jit(solution)/shard_map/all_to_all | solution.py:474
  15.6 0.1 faces.5
  15.6 0.0 copy-start
  15.6 9.8 %all_to_all.51.recv2_ref = f32[4,32,128]{2,1,0:T(8,128)S(1)} all-to-all(f32[4,32,128]{2,1,0:T(8,128)S(1)} %faces.5), channel_id=1, replica_groups={{756,0,12,24},{36,48,60,72},{84,96,108,120},{132,144,156,168},{180,192,..., dimensions={0} | all-to-all | bytes 131072 | tf_op jit(solution)/shard_map/all_to_all | solution.py:474
  25.4 0.0 copy-done
  25.4 1.2 %first.1 = (f32[512,128]{1,0:T(8,128)S(1)}, f32[512,128]{1,0:T(8,128)S(1)}, f32[512,128]{1,0:T(8,128)S(1)}, f32[512,128]{1,0:T(8,128)S(1)}, f32[4,16,128]{2,1,0:T(8,128)S(1)}, /*index=5*/f32[4,16,128]{2,1,0:T(8,128)S(1)}) custom-call(f32[2,512,128]{2,1,0:T(8,128)S(1)} %get-tuple-element.31.parts_ref, f32[4,32,128]{2,1,0:T(8,128)S(1)} %all_to_all.50.recv_ref, ...), custom_call_target="tpu_custom_call" | custom-call | tf_op jit(solution)/shard_map/first/pallas_call | solution.py:434
  26.6 9.2 %all_to_all.52.recv_ref = f32[4,16,128]{2,1,0:T(8,128)S(1)} all-to-all(f32[4,16,128]{2,1,0:T(8,128)S(1)} %get-tuple-element.36), channel_id=1, replica_groups={{756,0,12,24},{36,48,60,72},{84,96,108,120},{132,144,156,168},{180,192,..., dimensions={0} | all-to-all | bytes 65536 | tf_op jit(solution)/shard_map/all_to_all | solution.py:474
  35.9 0.1 faces.6
  36.0 5.8 %all_to_all.53.recv2_ref = f32[4,16,128]{2,1,0:T(8,128)S(1)} all-to-all(f32[4,16,128]{2,1,0:T(8,128)S(1)} %faces.6), channel_id=1, replica_groups={{0,1,12,13},{2,3,14,15},{4,5,16,17},{6,7,18,19},{8,9,20,21},{10,11,22,2..., dimensions={0} | all-to-all | bytes 65536 | tf_op jit(solution)/shard_map/all_to_all | solution.py:474
  41.7 1.2 %step.3 = (f32[512,128]{1,0:T(8,128)S(1)}, f32[512,128]{1,0:T(8,128)S(1)}, f32[512,128]{1,0:T(8,128)S(1)}, f32[4,16,128]{2,1,0:T(8,128)S(1)}, f32[4,16,128]{2,1,0:T(8,128)S(1)}) custom-call(f32[512,128]{1,0:T(8,128)S(1)} %get-tuple-element.35.part_ref, f32[4,16,128]{2,1,0:T(8,128)S(1)} %all_to_all.52.recv_ref, f32[4,16,128]{2,1,0:T(8,128)S(1)} %all_to_all.53.recv2_ref, ...), custom_call_target="tpu_custom_call" | custom-call | tf_op jit(solution)/shard_map/step/pallas_call | solution.py:434
  42.9 6.3 %all_to_all.54.recv_ref = f32[4,16,128]{2,1,0:T(8,128)S(1)} all-to-all(f32[4,16,128]{2,1,0:T(8,128)S(1)} %get-tuple-element.42), channel_id=1, replica_groups={{0,1,12,13},{2,3,14,15},{4,5,16,17},{6,7,18,19},{8,9,20,21},{10,11,22,2..., dimensions={0} | all-to-all | bytes 65536 | tf_op jit(solution)/shard_map/all_to_all | solution.py:474
  49.2 0.1 faces.7
  49.3 13.4 %all_to_all.55.recv2_ref = f32[4,16,128]{2,1,0:T(8,128)S(1)} all-to-all(f32[4,16,128]{2,1,0:T(8,128)S(1)} %faces.7), channel_id=1, replica_groups={{756,0,12,24},{36,48,60,72},{84,96,108,120},{132,144,156,168},{180,192,..., dimensions={0} | all-to-all | bytes 65536 | tf_op jit(solution)/shard_map/all_to_all | solution.py:474
  62.7 1.2 %step.4 = (f32[512,128]{1,0:T(8,128)S(1)}, f32[512,128]{1,0:T(8,128)S(1)}, f32[512,128]{1,0:T(8,128)S(1)}, f32[4,16,128]{2,1,0:T(8,128)S(1)}, f32[4,16,128]{2,1,0:T(8,128)S(1)}) custom-call(f32[512,128]{1,0:T(8,128)S(1)} %get-tuple-element.41.part_ref, f32[4,16,128]{2,1,0:T(8,128)S(1)} %all_to_all.54.recv_ref, f32[4,16,128]{2,1,0:T(8,128)S(1)} %all_to_all.55.recv2_ref, ...), custom_call_target="tpu_custom_call" | custom-call | tf_op jit(solution)/shard_map/step/pallas_call | solution.py:434
  63.9 9.2 %all_to_all.56.recv_ref = f32[4,16,128]{2,1,0:T(8,128)S(1)} all-to-all(f32[4,16,128]{2,1,0:T(8,128)S(1)} %get-tuple-element.47), channel_id=1, replica_groups={{756,0,12,24},{36,48,60,72},{84,96,108,120},{132,144,156,168},{180,192,..., dimensions={0} | all-to-all | bytes 65536 | tf_op jit(solution)/shard_map/all_to_all | solution.py:474
  73.1 0.1 faces.8
  73.2 4.9 %all_to_all.57.recv2_ref = f32[4,16,128]{2,1,0:T(8,128)S(1)} all-to-all(f32[4,16,128]{2,1,0:T(8,128)S(1)} %faces.8), channel_id=1, replica_groups={{0,1,12,13},{2,3,14,15},{4,5,16,17},{6,7,18,19},{8,9,20,21},{10,11,22,2..., dimensions={0} | all-to-all | bytes 65536 | tf_op jit(solution)/shard_map/all_to_all | solution.py:474
  78.1 1.2 %step.5 = (f32[512,128]{1,0:T(8,128)S(1)}, f32[512,128]{1,0:T(8,128)S(1)}, f32[512,128]{1,0:T(8,128)S(1)}, f32[4,16,128]{2,1,0:T(8,128)S(1)}, f32[4,16,128]{2,1,0:T(8,128)S(1)}) custom-call(f32[512,128]{1,0:T(8,128)S(1)} %get-tuple-element.46.part_ref, f32[4,16,128]{2,1,0:T(8,128)S(1)} %all_to_all.56.recv_ref, f32[4,16,128]{2,1,0:T(8,128)S(1)} %all_to_all.57.recv2_ref, ...), custom_call_target="tpu_custom_call" | custom-call | tf_op jit(solution)/shard_map/step/pallas_call | solution.py:434
  79.3 6.3 %all_to_all.58.recv_ref = f32[4,16,128]{2,1,0:T(8,128)S(1)} all-to-all(f32[4,16,128]{2,1,0:T(8,128)S(1)} %get-tuple-element.52), channel_id=1, replica_groups={{0,1,12,13},{2,3,14,15},{4,5,16,17},{6,7,18,19},{8,9,20,21},{10,11,22,2..., dimensions={0} | all-to-all | bytes 65536 | tf_op jit(solution)/shard_map/all_to_all | solution.py:474
  85.6 0.1 faces.9
  85.7 16.6 %all_to_all.59.recv2_ref = f32[4,16,128]{2,1,0:T(8,128)S(1)} all-to-all(f32[4,16,128]{2,1,0:T(8,128)S(1)} %faces.9), channel_id=1, replica_groups={{756,0,12,24},{36,48,60,72},{84,96,108,120},{132,144,156,168},{180,192,..., dimensions={0} | all-to-all | bytes 65536 | tf_op jit(solution)/shard_map/all_to_all | solution.py:474
  102.2 1.1 %end.1 = f32[512,128]{1,0:T(8,128)} custom-call(f32[512,128]{1,0:T(8,128)S(1)} %get-tuple-element.51.part_ref, f32[4,16,128]{2,1,0:T(8,128)S(1)} %all_to_all.58.recv_ref, f32[4,16,128]{2,1,0:T(8,128)S(1)} %all_to_all.59.recv2_ref, f32[512,128]{1,0:T(8,128)S(1)} %get-tuple-element.54.residual_ref, f32[512,128]{1,0:T(8,128)S(1)} %get-tuple-element.39.diag_ref, ...), custom_call_target="tpu_custom_call" | custom-call | tf_op jit(solution)/shard_map/end/pallas_call | solution.py:434
Async XLA Ops:
  15.6 9.8 %copy-start = (bf16[128,192]{1,0:T(8,128)(2,1)S(1)}, bf16[128,192]{1,0:T(8,128)(2,1)}, u32[]{:S(2)}) copy-start(bf16[128,192]{1,0:T(8,128)(2,1)} %constant.4.clone.table_ref) | copy-start | bytes 147460

commit v3 on v2

--- a/solution.py
+++ b/solution.py
@@ -14,6 +14,7 @@
 ORDERS = ((0, 1), (1, 0), (0, 1), (1, 0), (0, 1))
 LANES = 128
 ROWS = NP**3
+ROOM = ROWS + 8
 
 cheb_low = 0.4
 cheb_high = 4.0
@@ -383,8 +384,8 @@
 
 def first_kernel(sizes, before, order, centre, parts_ref, recv_ref, recv2_ref, geo_ref, table_ref, residual_ref, diag_ref, direction_ref, image_ref, send_ref, later_ref, work_ref):
     sides = two_sides(sizes, before)
-    residual_ref[...] = parts_ref[0]
-    diag_ref[...] = parts_ref[1]
+    residual_ref[...] = parts_ref[0, 0:ROWS, :]
+    diag_ref[...] = parts_ref[1, 0:ROWS, :]
     for field, ref in ((0, residual_ref), (1, diag_ref)):
         add_faces(ref, recv_ref, field, sides[0])
         add_faces(ref, recv2_ref, field, sides[1])
@@ -396,7 +397,7 @@
 
 def step_kernel(sizes, before, order, pair, part_ref, recv_ref, recv2_ref, geo_ref, table_ref, old_residual_ref, diag_ref, old_direction_ref, residual_ref, direction_ref, image_ref, send_ref, later_ref, work_ref):
     sides = two_sides(sizes, before)
-    work_ref[...] = part_ref[...]
+    work_ref[...] = part_ref[0:ROWS, :]
     add_faces(work_ref, recv_ref, 0, sides[0])
     add_faces(work_ref, recv2_ref, 0, sides[1])
     residual = old_residual_ref[...] - work_ref[...]
@@ -409,7 +410,7 @@
 
 def end_kernel(sizes, before, pair, part_ref, recv_ref, recv2_ref, residual_ref, diag_ref, d0_ref, d1_ref, d2_ref, d3_ref, one_hot_ref, out_hbm, work_ref, out_ref, sems):
     sides = two_sides(sizes, before)
-    work_ref[...] = part_ref[...]
+    work_ref[...] = part_ref[0:ROWS, :]
     add_faces(work_ref, recv_ref, 0, sides[0])
     add_faces(work_ref, recv2_ref, 0, sides[1])
     table = one_hot_ref[...]
@@ -462,6 +463,7 @@
     apply_table, diag_table, square, middle = tables()
     centre, steps = coefficients()
     field = jax.ShapeDtypeStruct((ROWS, LANES), jnp.float32)
+    sums = jax.ShapeDtypeStruct((ROOM, LANES), jnp.float32)
     one = jax.ShapeDtypeStruct((4, 16, LANES), jnp.float32)
     two = jax.ShapeDtypeStruct((4, 32, LANES), jnp.float32)
 
@@ -494,7 +496,7 @@
             functools.partial(begin_kernel, sizes, orders[0], square, middle),
             (
                 jax.ShapeDtypeStruct(geometry.shape, jnp.bfloat16),
-                jax.ShapeDtypeStruct((2, ROWS, LANES), jnp.float32),
+                jax.ShapeDtypeStruct((2, ROOM, LANES), jnp.float32),
                 jax.ShapeDtypeStruct((LANES, LANES), jnp.bfloat16),
                 two,
                 two,
@@ -517,7 +519,7 @@
         recv, recv2 = assemble(send, later, orders[0], 2)
         residual, diag, direction, image, send, later = call(
             functools.partial(first_kernel, sizes, orders[0], orders[1], centre),
-            (field, field, field, field, one, one),
+            (field, field, field, sums, one, one),
             parts,
             recv,
             recv2,
@@ -531,7 +533,7 @@
             recv, recv2 = assemble(send, later, orders[step + 1], 1)
             residual, direction, image, send, later = call(
                 functools.partial(step_kernel, sizes, orders[step + 1], orders[step + 2], pair),
-                (field, field, field, one, one),
+                (field, field, sums, one, one),
                 image,
                 recv,
                 recv2,

time: 104 us -> 104 us (level)
  no operation moved by 1% of the time
where the time goes in v3:
time: 104 us
  blocking collectives  94.7 us (91%)
  Pallas kernels  8.83 us (8%)
    all_to_all x10, blocking collectives, exchange(): lax.all_to_all(send, ('dom', 'sub'), 0, 0, axis_index_groups=exchange_gro...  94.7 us
    pallas_call x11, Pallas kernels, call(): pl.pallas_call(kernel, out_shape=outs, scratch_shapes=list(scratch), comp...  8.83 us

profile of v3, /device:TPU:64, one launch (start us, length us, event | category | flops | bytes accessed | tf_op | source)
XLA Modules:
  0.0 103.5 jit_solution(13371153222184759206)
XLA Ops:
  0.0 2.4 %begin.1 = (bf16[6,512,128]{2,1,0:T(8,128)(2,1)S(1)}, f32[2,520,128]{2,1,0:T(8,128)S(1)}, bf16[128,128]{1,0:T(8,128)(2,1)S(1)}, f32[4,32,128]{2,1,0:T(8,128)S(1)}, f32[4,32,128]{2,1,0:T(8,128)S(1)}) custom-call(bf16[6,512,128]{2,1,0:T(8,128)(2,1)} %geo_hbm.1, f32[512,128]{1,0:T(8,128)} %load_hbm.1, s32[1,128]{1,0:T(1,128)} %cells_hbm.1, ...), custom_call_target="tpu_custom_call" | custom-call | tf_op jit(solution)/shard_map/begin/pallas_call | solution.py:435
  2.4 13.1 %all_to_all.50.recv_ref = f32[4,32,128]{2,1,0:T(8,128)S(1)} all-to-all(f32[4,32,128]{2,1,0:T(8,128)S(1)} %get-tuple-element.32), channel_id=1, replica_groups={{0,1,12,13},{2,3,14,15},{4,5,16,17},{6,7,18,19},{8,9,20,21},{10,11,22,2..., dimensions={0} | all-to-all | bytes 131072 | tf_op jit(solution)/shard_map/all_to_all | solution.py:476
  15.6 0.1 faces.5
  15.7 0.0 copy-start
  15.7 9.8 %all_to_all.51.recv2_ref = f32[4,32,128]{2,1,0:T(8,128)S(1)} all-to-all(f32[4,32,128]{2,1,0:T(8,128)S(1)} %faces.5), channel_id=1, replica_groups={{756,0,12,24},{36,48,60,72},{84,96,108,120},{132,144,156,168},{180,192,..., dimensions={0} | all-to-all | bytes 131072 | tf_op jit(solution)/shard_map/all_to_all | solution.py:476
  25.5 0.0 copy-done
  25.5 1.2 %first.1 = (f32[512,128]{1,0:T(8,128)S(1)}, f32[512,128]{1,0:T(8,128)S(1)}, f32[512,128]{1,0:T(8,128)S(1)}, f32[520,128]{1,0:T(8,128)S(1)}, f32[4,16,128]{2,1,0:T(8,128)S(1)}, /*index=5*/f32[4,16,128]{2,1,0:T(8,128)S(1)}) custom-call(f32[2,520,128]{2,1,0:T(8,128)S(1)} %get-tuple-element.31.parts_ref, f32[4,32,128]{2,1,0:T(8,128)S(1)} %all_to_all.50.recv_ref, ...), custom_call_target="tpu_custom_call" | custom-call | tf_op jit(solution)/shard_map/first/pallas_call | solution.py:435
  26.7 9.2 %all_to_all.52.recv_ref = f32[4,16,128]{2,1,0:T(8,128)S(1)} all-to-all(f32[4,16,128]{2,1,0:T(8,128)S(1)} %get-tuple-element.36), channel_id=1, replica_groups={{756,0,12,24},{36,48,60,72},{84,96,108,120},{132,144,156,168},{180,192,..., dimensions={0} | all-to-all | bytes 65536 | tf_op jit(solution)/shard_map/all_to_all | solution.py:476
  35.9 0.1 faces.6
  36.0 5.8 %all_to_all.53.recv2_ref = f32[4,16,128]{2,1,0:T(8,128)S(1)} all-to-all(f32[4,16,128]{2,1,0:T(8,128)S(1)} %faces.6), channel_id=1, replica_groups={{0,1,12,13},{2,3,14,15},{4,5,16,17},{6,7,18,19},{8,9,20,21},{10,11,22,2..., dimensions={0} | all-to-all | bytes 65536 | tf_op jit(solution)/shard_map/all_to_all | solution.py:476
  41.8 1.2 %step.3 = (f32[512,128]{1,0:T(8,128)S(1)}, f32[512,128]{1,0:T(8,128)S(1)}, f32[520,128]{1,0:T(8,128)S(1)}, f32[4,16,128]{2,1,0:T(8,128)S(1)}, f32[4,16,128]{2,1,0:T(8,128)S(1)}) custom-call(f32[520,128]{1,0:T(8,128)S(1)} %get-tuple-element.35.part_ref, f32[4,16,128]{2,1,0:T(8,128)S(1)} %all_to_all.52.recv_ref, f32[4,16,128]{2,1,0:T(8,128)S(1)} %all_to_all.53.recv2_ref, ...), custom_call_target="tpu_custom_call" | custom-call | tf_op jit(solution)/shard_map/step/pallas_call | solution.py:435
  43.0 6.3 %all_to_all.54.recv_ref = f32[4,16,128]{2,1,0:T(8,128)S(1)} all-to-all(f32[4,16,128]{2,1,0:T(8,128)S(1)} %get-tuple-element.42), channel_id=1, replica_groups={{0,1,12,13},{2,3,14,15},{4,5,16,17},{6,7,18,19},{8,9,20,21},{10,11,22,2..., dimensions={0} | all-to-all | bytes 65536 | tf_op jit(solution)/shard_map/all_to_all | solution.py:476
  49.3 0.1 faces.7
  49.3 13.4 %all_to_all.55.recv2_ref = f32[4,16,128]{2,1,0:T(8,128)S(1)} all-to-all(f32[4,16,128]{2,1,0:T(8,128)S(1)} %faces.7), channel_id=1, replica_groups={{756,0,12,24},{36,48,60,72},{84,96,108,120},{132,144,156,168},{180,192,..., dimensions={0} | all-to-all | bytes 65536 | tf_op jit(solution)/shard_map/all_to_all | solution.py:476
  62.8 1.2 %step.4 = (f32[512,128]{1,0:T(8,128)S(1)}, f32[512,128]{1,0:T(8,128)S(1)}, f32[520,128]{1,0:T(8,128)S(1)}, f32[4,16,128]{2,1,0:T(8,128)S(1)}, f32[4,16,128]{2,1,0:T(8,128)S(1)}) custom-call(f32[520,128]{1,0:T(8,128)S(1)} %get-tuple-element.41.part_ref, f32[4,16,128]{2,1,0:T(8,128)S(1)} %all_to_all.54.recv_ref, f32[4,16,128]{2,1,0:T(8,128)S(1)} %all_to_all.55.recv2_ref, ...), custom_call_target="tpu_custom_call" | custom-call | tf_op jit(solution)/shard_map/step/pallas_call | solution.py:435
  64.0 9.2 %all_to_all.56.recv_ref = f32[4,16,128]{2,1,0:T(8,128)S(1)} all-to-all(f32[4,16,128]{2,1,0:T(8,128)S(1)} %get-tuple-element.47), channel_id=1, replica_groups={{756,0,12,24},{36,48,60,72},{84,96,108,120},{132,144,156,168},{180,192,..., dimensions={0} | all-to-all | bytes 65536 | tf_op jit(solution)/shard_map/all_to_all | solution.py:476
  73.2 0.1 faces.8
  73.3 4.9 %all_to_all.57.recv2_ref = f32[4,16,128]{2,1,0:T(8,128)S(1)} all-to-all(f32[4,16,128]{2,1,0:T(8,128)S(1)} %faces.8), channel_id=1, replica_groups={{0,1,12,13},{2,3,14,15},{4,5,16,17},{6,7,18,19},{8,9,20,21},{10,11,22,2..., dimensions={0} | all-to-all | bytes 65536 | tf_op jit(solution)/shard_map/all_to_all | solution.py:476
  78.2 1.2 %step.5 = (f32[512,128]{1,0:T(8,128)S(1)}, f32[512,128]{1,0:T(8,128)S(1)}, f32[520,128]{1,0:T(8,128)S(1)}, f32[4,16,128]{2,1,0:T(8,128)S(1)}, f32[4,16,128]{2,1,0:T(8,128)S(1)}) custom-call(f32[520,128]{1,0:T(8,128)S(1)} %get-tuple-element.46.part_ref, f32[4,16,128]{2,1,0:T(8,128)S(1)} %all_to_all.56.recv_ref, f32[4,16,128]{2,1,0:T(8,128)S(1)} %all_to_all.57.recv2_ref, ...), custom_call_target="tpu_custom_call" | custom-call | tf_op jit(solution)/shard_map/step/pallas_call | solution.py:435
  79.4 6.3 %all_to_all.58.recv_ref = f32[4,16,128]{2,1,0:T(8,128)S(1)} all-to-all(f32[4,16,128]{2,1,0:T(8,128)S(1)} %get-tuple-element.52), channel_id=1, replica_groups={{0,1,12,13},{2,3,14,15},{4,5,16,17},{6,7,18,19},{8,9,20,21},{10,11,22,2..., dimensions={0} | all-to-all | bytes 65536 | tf_op jit(solution)/shard_map/all_to_all | solution.py:476
  85.7 0.1 faces.9
  85.8 16.6 %all_to_all.59.recv2_ref = f32[4,16,128]{2,1,0:T(8,128)S(1)} all-to-all(f32[4,16,128]{2,1,0:T(8,128)S(1)} %faces.9), channel_id=1, replica_groups={{756,0,12,24},{36,48,60,72},{84,96,108,120},{132,144,156,168},{180,192,..., dimensions={0} | all-to-all | bytes 65536 | tf_op jit(solution)/shard_map/all_to_all | solution.py:476
  102.4 1.2 %end.1 = f32[512,128]{1,0:T(8,128)} custom-call(f32[520,128]{1,0:T(8,128)S(1)} %get-tuple-element.51.part_ref, f32[4,16,128]{2,1,0:T(8,128)S(1)} %all_to_all.58.recv_ref, f32[4,16,128]{2,1,0:T(8,128)S(1)} %all_to_all.59.recv2_ref, f32[512,128]{1,0:T(8,128)S(1)} %get-tuple-element.54.residual_ref, f32[512,128]{1,0:T(8,128)S(1)} %get-tuple-element.39.diag_ref, ...), custom_call_target="tpu_custom_call" | custom-call | tf_op jit(solution)/shard_map/end/pallas_call | solution.py:435
Async XLA Ops:
  15.7 9.8 %copy-start = (bf16[128,192]{1,0:T(8,128)(2,1)S(1)}, bf16[128,192]{1,0:T(8,128)(2,1)}, u32[]{:S(2)}) copy-start(bf16[128,192]{1,0:T(8,128)(2,1)} %constant.4.clone.table_ref) | copy-start | bytes 147460

commit v4 on v3

--- a/solution.py
+++ b/solution.py
@@ -67,7 +67,7 @@
     inner_t = three_products(np.kron(eye, derivative.T))
     apply_table = np.concatenate([inner, inner_t], axis=0)
     square = derivative * derivative
-    diag_table = three_products(np.kron(eye, square.T))
+    diag_table = three_products(np.kron(eye, square.T))[:, ROWS // 8 :]
     rows = [[float(v) for v in row] for row in square.T]
     return apply_table, diag_table, rows, [float(v) for v in np.diagonal(derivative)]
 
@@ -277,9 +277,9 @@
     write_faces(later_ref, field, pack_faces(ref, sides[1]), sides[1])
 
 
-def permute_exact(values, table):
+def permute_parts(values, table):
     total = None
-    for part in range(3):
+    for part in range(2):
         piece = values.astype(jnp.bfloat16)
         moved = multiply(piece, table)
         values = values - piece.astype(jnp.float32)
@@ -324,7 +324,7 @@
     third = jnp.where(sub_row == 0, middle[0], jnp.where(sub_row == 7, middle[7], 0.0))
     for i in range(NP):
         at = slice(i * 64, i * 64 + 64)
-        load_part[at, :] = permute_exact(load_ref[at, :], table)
+        load_part[at, :] = permute_parts(load_ref[at, :], table)
         second = geo_out[1, at, :].astype(jnp.float32)
         fifth = geo_out[5, at, :].astype(jnp.float32)
         pieces = blend([second[j * 8 : j * 8 + 8, :] for j in range(NP)], square)
@@ -335,7 +335,8 @@
                 extra = extra + middle[i] * middle[j] * cross
             pieces[j] = pieces[j] + 2.0 * extra
         total = jnp.concatenate(pieces, axis=0)
-        total = total + multiply(inner, split_rows(geo_out[2, at, :].astype(jnp.float32)))
+        along = geo_out[2, at, :]
+        total = total + multiply(inner, jnp.concatenate([along, along], axis=0))
         if i in (0, 7):
             total = total + 2.0 * middle[i] * third * geo_out[4, at, :].astype(jnp.float32)
         diag_part[at, :] = diag_part[at, :] + total
@@ -421,7 +422,7 @@
         last = d3_ref[at, :]
         direction = pair[0] * last + pair[1] * (residual / diag_ref[at, :])
         iterate = d0_ref[at, :] + d1_ref[at, :] + d2_ref[at, :] + last + direction
-        out_ref[at, :] = permute_exact(iterate, table)
+        out_ref[at, :] = permute_parts(iterate, table)
         if i % 2 == 1:
             here = pl.ds((i - 1) * 64, 128)
             copy = pltpu.make_async_copy(out_ref.at[here], out_hbm.at[here], sems.at[i // 2])

time: 104 us -> 104 us (level)
  no operation moved by 1% of the time
where the time goes in v4:
time: 104 us; the launch traced here: 103 us
  blocking collectives  94.7 us (91%)
  Pallas kernels  8.65 us (8%)
    all_to_all x10, blocking collectives, exchange(): lax.all_to_all(send, ('dom', 'sub'), 0, 0, axis_index_groups=exchange_gro...  94.7 us
    pallas_call x11, Pallas kernels, call(): pl.pallas_call(kernel, out_shape=outs, scratch_shapes=list(scratch), comp...  8.65 us

profile of v4, /device:TPU:64, one launch (start us, length us, event | category | flops | bytes accessed | tf_op | source)
XLA Modules:
  0.0 103.4 jit_solution(3796929649523450780)
XLA Ops:
  0.0 2.3 %begin.1 = (bf16[6,512,128]{2,1,0:T(8,128)(2,1)S(1)}, f32[2,520,128]{2,1,0:T(8,128)S(1)}, bf16[128,128]{1,0:T(8,128)(2,1)S(1)}, f32[4,32,128]{2,1,0:T(8,128)S(1)}, f32[4,32,128]{2,1,0:T(8,128)S(1)}) custom-call(bf16[6,512,128]{2,1,0:T(8,128)(2,1)} %geo_hbm.1, f32[512,128]{1,0:T(8,128)} %load_hbm.1, s32[1,128]{1,0:T(1,128)} %cells_hbm.1, ...), custom_call_target="tpu_custom_call" | custom-call | tf_op jit(solution)/shard_map/begin/pallas_call | solution.py:436
  2.3 13.1 %all_to_all.50.recv_ref = f32[4,32,128]{2,1,0:T(8,128)S(1)} all-to-all(f32[4,32,128]{2,1,0:T(8,128)S(1)} %get-tuple-element.32), channel_id=1, replica_groups={{0,1,12,13},{2,3,14,15},{4,5,16,17},{6,7,18,19},{8,9,20,21},{10,11,22,2..., dimensions={0} | all-to-all | bytes 131072 | tf_op jit(solution)/shard_map/all_to_all | solution.py:477
  15.5 0.1 faces.5
  15.5 0.0 copy-start
  15.5 9.8 %all_to_all.51.recv2_ref = f32[4,32,128]{2,1,0:T(8,128)S(1)} all-to-all(f32[4,32,128]{2,1,0:T(8,128)S(1)} %faces.5), channel_id=1, replica_groups={{756,0,12,24},{36,48,60,72},{84,96,108,120},{132,144,156,168},{180,192,..., dimensions={0} | all-to-all | bytes 131072 | tf_op jit(solution)/shard_map/all_to_all | solution.py:477
  25.3 0.0 copy-done
  25.3 1.2 %first.1 = (f32[512,128]{1,0:T(8,128)S(1)}, f32[512,128]{1,0:T(8,128)S(1)}, f32[512,128]{1,0:T(8,128)S(1)}, f32[520,128]{1,0:T(8,128)S(1)}, f32[4,16,128]{2,1,0:T(8,128)S(1)}, /*index=5*/f32[4,16,128]{2,1,0:T(8,128)S(1)}) custom-call(f32[2,520,128]{2,1,0:T(8,128)S(1)} %get-tuple-element.31.parts_ref, f32[4,32,128]{2,1,0:T(8,128)S(1)} %all_to_all.50.recv_ref, ...), custom_call_target="tpu_custom_call" | custom-call | tf_op jit(solution)/shard_map/first/pallas_call | solution.py:436
  26.6 9.2 %all_to_all.52.recv_ref = f32[4,16,128]{2,1,0:T(8,128)S(1)} all-to-all(f32[4,16,128]{2,1,0:T(8,128)S(1)} %get-tuple-element.36), channel_id=1, replica_groups={{756,0,12,24},{36,48,60,72},{84,96,108,120},{132,144,156,168},{180,192,..., dimensions={0} | all-to-all | bytes 65536 | tf_op jit(solution)/shard_map/all_to_all | solution.py:477
  35.8 0.1 faces.6
  35.9 5.8 %all_to_all.53.recv2_ref = f32[4,16,128]{2,1,0:T(8,128)S(1)} all-to-all(f32[4,16,128]{2,1,0:T(8,128)S(1)} %faces.6), channel_id=1, replica_groups={{0,1,12,13},{2,3,14,15},{4,5,16,17},{6,7,18,19},{8,9,20,21},{10,11,22,2..., dimensions={0} | all-to-all | bytes 65536 | tf_op jit(solution)/shard_map/all_to_all | solution.py:477
  41.6 1.2 %step.3 = (f32[512,128]{1,0:T(8,128)S(1)}, f32[512,128]{1,0:T(8,128)S(1)}, f32[520,128]{1,0:T(8,128)S(1)}, f32[4,16,128]{2,1,0:T(8,128)S(1)}, f32[4,16,128]{2,1,0:T(8,128)S(1)}) custom-call(f32[520,128]{1,0:T(8,128)S(1)} %get-tuple-element.35.part_ref, f32[4,16,128]{2,1,0:T(8,128)S(1)} %all_to_all.52.recv_ref, f32[4,16,128]{2,1,0:T(8,128)S(1)} %all_to_all.53.recv2_ref, ...), custom_call_target="tpu_custom_call" | custom-call | tf_op jit(solution)/shard_map/step/pallas_call | solution.py:436
  42.9 6.3 %all_to_all.54.recv_ref = f32[4,16,128]{2,1,0:T(8,128)S(1)} all-to-all(f32[4,16,128]{2,1,0:T(8,128)S(1)} %get-tuple-element.42), channel_id=1, replica_groups={{0,1,12,13},{2,3,14,15},{4,5,16,17},{6,7,18,19},{8,9,20,21},{10,11,22,2..., dimensions={0} | all-to-all | bytes 65536 | tf_op jit(solution)/shard_map/all_to_all | solution.py:477
  49.2 0.1 faces.7
  49.2 13.4 %all_to_all.55.recv2_ref = f32[4,16,128]{2,1,0:T(8,128)S(1)} all-to-all(f32[4,16,128]{2,1,0:T(8,128)S(1)} %faces.7), channel_id=1, replica_groups={{756,0,12,24},{36,48,60,72},{84,96,108,120},{132,144,156,168},{180,192,..., dimensions={0} | all-to-all | bytes 65536 | tf_op jit(solution)/shard_map/all_to_all | solution.py:477
  62.7 1.2 %step.4 = (f32[512,128]{1,0:T(8,128)S(1)}, f32[512,128]{1,0:T(8,128)S(1)}, f32[520,128]{1,0:T(8,128)S(1)}, f32[4,16,128]{2,1,0:T(8,128)S(1)}, f32[4,16,128]{2,1,0:T(8,128)S(1)}) custom-call(f32[520,128]{1,0:T(8,128)S(1)} %get-tuple-element.41.part_ref, f32[4,16,128]{2,1,0:T(8,128)S(1)} %all_to_all.54.recv_ref, f32[4,16,128]{2,1,0:T(8,128)S(1)} %all_to_all.55.recv2_ref, ...), custom_call_target="tpu_custom_call" | custom-call | tf_op jit(solution)/shard_map/step/pallas_call | solution.py:436
  63.9 9.2 %all_to_all.56.recv_ref = f32[4,16,128]{2,1,0:T(8,128)S(1)} all-to-all(f32[4,16,128]{2,1,0:T(8,128)S(1)} %get-tuple-element.47), channel_id=1, replica_groups={{756,0,12,24},{36,48,60,72},{84,96,108,120},{132,144,156,168},{180,192,..., dimensions={0} | all-to-all | bytes 65536 | tf_op jit(solution)/shard_map/all_to_all | solution.py:477
  73.1 0.1 faces.8
  73.2 4.9 %all_to_all.57.recv2_ref = f32[4,16,128]{2,1,0:T(8,128)S(1)} all-to-all(f32[4,16,128]{2,1,0:T(8,128)S(1)} %faces.8), channel_id=1, replica_groups={{0,1,12,13},{2,3,14,15},{4,5,16,17},{6,7,18,19},{8,9,20,21},{10,11,22,2..., dimensions={0} | all-to-all | bytes 65536 | tf_op jit(solution)/shard_map/all_to_all | solution.py:477
  78.1 1.2 %step.5 = (f32[512,128]{1,0:T(8,128)S(1)}, f32[512,128]{1,0:T(8,128)S(1)}, f32[520,128]{1,0:T(8,128)S(1)}, f32[4,16,128]{2,1,0:T(8,128)S(1)}, f32[4,16,128]{2,1,0:T(8,128)S(1)}) custom-call(f32[520,128]{1,0:T(8,128)S(1)} %get-tuple-element.46.part_ref, f32[4,16,128]{2,1,0:T(8,128)S(1)} %all_to_all.56.recv_ref, f32[4,16,128]{2,1,0:T(8,128)S(1)} %all_to_all.57.recv2_ref, ...), custom_call_target="tpu_custom_call" | custom-call | tf_op jit(solution)/shard_map/step/pallas_call | solution.py:436
  79.3 6.3 %all_to_all.58.recv_ref = f32[4,16,128]{2,1,0:T(8,128)S(1)} all-to-all(f32[4,16,128]{2,1,0:T(8,128)S(1)} %get-tuple-element.52), channel_id=1, replica_groups={{0,1,12,13},{2,3,14,15},{4,5,16,17},{6,7,18,19},{8,9,20,21},{10,11,22,2..., dimensions={0} | all-to-all | bytes 65536 | tf_op jit(solution)/shard_map/all_to_all | solution.py:477
  85.6 0.1 faces.9
  85.7 16.6 %all_to_all.59.recv2_ref = f32[4,16,128]{2,1,0:T(8,128)S(1)} all-to-all(f32[4,16,128]{2,1,0:T(8,128)S(1)} %faces.9), channel_id=1, replica_groups={{756,0,12,24},{36,48,60,72},{84,96,108,120},{132,144,156,168},{180,192,..., dimensions={0} | all-to-all | bytes 65536 | tf_op jit(solution)/shard_map/all_to_all | solution.py:477
  102.3 1.1 %end.1 = f32[512,128]{1,0:T(8,128)} custom-call(f32[520,128]{1,0:T(8,128)S(1)} %get-tuple-element.51.part_ref, f32[4,16,128]{2,1,0:T(8,128)S(1)} %all_to_all.58.recv_ref, f32[4,16,128]{2,1,0:T(8,128)S(1)} %all_to_all.59.recv2_ref, f32[512,128]{1,0:T(8,128)S(1)} %get-tuple-element.54.residual_ref, f32[512,128]{1,0:T(8,128)S(1)} %get-tuple-element.39.diag_ref, ...), custom_call_target="tpu_custom_call" | custom-call | tf_op jit(solution)/shard_map/end/pallas_call | solution.py:436
Async XLA Ops:
  15.5 9.8 %copy-start = (bf16[128,192]{1,0:T(8,128)(2,1)S(1)}, bf16[128,192]{1,0:T(8,128)(2,1)}, u32[]{:S(2)}) copy-start(bf16[128,192]{1,0:T(8,128)(2,1)} %constant.4.clone.table_ref) | copy-start | bytes 147460
